TPU v7x, 1024 devices: a whole 4x8x16 slice. The times are simulated.
1024 devices in a mesh: island: 16 (over z_lo, core), dev: 64 (over x, y, z_hi).
Axes of the slice: x: 4, y: 8, z: 16 (z_hi: 2, z_lo: 8; z = z_hi * 8 + z_lo), core: 2. Of those that a mesh axis runs over, the one named last changes fastest.
Arguments:
- image_embed: bfloat16 [262144, 1152], P(('island', 'dev')), may hold values from -6 to 6
- text_feat: bfloat16 [262144, 1152], P(('island', 'dev')), may hold values from -1.1953125 to 1.1953125
- text_proj: bfloat16 [1152, 1152], P('dev'), may hold values from -0.1875 to 0.1875
- log_scale: float32 [], replicated, may hold values from 1.5 to 2.3
- bias: float32 [], replicated, may hold values from -3 to -1
Outputs:
- grad_text: bfloat16 [262144, 1152], P(('island', 'dev'))
All inputs are finite; a program needn't handle non-finite values.
Results may differ from a plain program's by a relative error of at most 0.0065.
Values may be sent and summed in bfloat16 or wider, within the bound.
No kernel may reach another device: no remote copies, remote signals or barrier semaphores. Data moves between devices by JAX's collectives and lax.ppermute only.
A program may use at most 32 MiB of HBM per device.

v0:
```python
import jax
import jax.numpy as jnp
from jax import lax
from jax.sharding import PartitionSpec as P

norm_eps = 1e-06


def passed_along(value, axis, by):
    count = lax.axis_size(axis)
    return lax.ppermute(value, axis, [(i, (i + by) % count) for i in range(count)])


def body(image_embed, text_feat, text_proj, log_scale, bias):
    row_count = text_feat.shape[0]
    feat_width = text_feat.shape[1]
    image_f = image_embed.astype(jnp.float32)
    unit_img = (
        image_f * lax.rsqrt(jnp.sum(image_f * image_f, axis=1, keepdims=True) + norm_eps)
    ).astype(jnp.bfloat16)
    full_proj = lax.all_gather(text_proj, "dev", axis=0, tiled=True)
    hidden = jnp.dot(text_feat, full_proj, preferred_element_type=jnp.float32)
    inv_norm = lax.rsqrt(jnp.sum(hidden * hidden, axis=1, keepdims=True) + norm_eps)
    unit_txt = hidden * inv_norm
    text_b = unit_txt.astype(jnp.bfloat16)
    logit_scale = jnp.exp(log_scale)
    turn_count = min(4, lax.axis_size("island"))
    own_pairs = jnp.eye(row_count, dtype=jnp.float32)
    moved_text = text_b
    partial_value = jnp.zeros((row_count, feat_width), jnp.float32)
    for turn in range(turn_count):
        scores = (
            logit_scale
            * lax.dot_general(
                moved_text, unit_img, (((1,), (1,)), ((), ())), preferred_element_type=jnp.float32
            )
            + bias
        )
        probs = jax.nn.sigmoid(scores)
        if turn == 0:
            probs = probs - own_pairs
        weights = probs.astype(jnp.bfloat16)
        partial_value = partial_value + logit_scale * jnp.dot(
            weights, unit_img, preferred_element_type=jnp.float32
        )
        if turn + 1 < turn_count:
            moved_text = passed_along(moved_text, "island", 1)
            partial_value = passed_along(partial_value, "island", 1)
    grad_unit = passed_along(partial_value, "island", 1 - turn_count)
    radial = jnp.sum(unit_txt * grad_unit, axis=1, keepdims=True)
    grad_hidden = ((grad_unit - unit_txt * radial) * inv_norm).astype(jnp.bfloat16)
    grad_text = lax.dot_general(
        grad_hidden, full_proj, (((1,), (1,)), ((), ())), preferred_element_type=jnp.float32
    )
    return grad_text.astype(jnp.bfloat16)


def solution(mesh):
    placed = (P(("island", "dev"), None), P(("island", "dev"), None), P("dev", None), P(), P())
    return jax.shard_map(
        body, mesh=mesh, in_specs=placed, out_specs=P(("island", "dev"), None), check_vma=False
    )
```

profile of v0, /device:TPU:1, one launch (start us, length us, event | category | flops | bytes accessed | tf_op | source)
XLA Modules:
  0.0 384.6 jit_solution(888279045422242962)
XLA Ops:
  6.5 0.0 copy-start
  6.5 0.0 all-gather.3.cloned.1.call-start
  6.5 0.7 all-gather.3.cloned.1.call-update
  8.6 1.3 fusion.1
  9.9 213.1 %all-gather.3.cloned.1.call-done = bf16[64,18,1152]{2,1,0:T(8,128)(2,1)} async-done(((bf16[1,18,1152]{2,1,0:T(8,128)(2,1)}), bf16[64,18,1152]{2,1,0:T(8,128)(2,1)}) %all-gather.3.cloned.1.call-update) | async-done | bytes 2654224 | tf_op jit(solution)/shard_map/all_gather | solution.py:21
  222.9 5.4 %reshape.14 = bf16[1152,1152]{1,0:T(8,128)(2,1)} reshape(bf16[64,18,1152]{2,1,0:T(8,128)(2,1)} %all-gather.3.cloned.1.call-done) | data formatting | bytes 5308416
  228.3 0.0 copy-done
  228.3 2.8 multiply_reduce_fusion.1
  231.1 0.0 copy-start.1
  231.2 0.1 multiply_convert_fusion.1
  231.3 0.0 copy-start.2
  231.3 0.8 copy-done.2
  232.1 0.1 copy-done.1
  232.2 2.0 convolution_multiply_fusion.3
  234.2 6.8 %collective-permute-start = (f32[256,1152]{1,0:T(8,128)}, f32[256,1152]{1,0:T(8,128)S(1)}, u32[]{:S(2)}, u32[]{:S(2)}) collective-permute-start(f32[256,1152]{1,0:T(8,128)} %convolution_multiply_fusion.3), channel_id=1, source_target_pairs={{0,64},{64,128},{128,192},{192,256},{256,320},{320,384},{384,448},... | collective-permute-start | bytes 3538952 | tf_op jit(solution)/shard_map/ppermute | solution.py:11
  241.0 1.9 collective-permute-start.1
  243.0 17.8 %collective-permute-done.1 = bf16[256,1152]{1,0:T(8,128)(2,1)} collective-permute-done((bf16[256,1152]{1,0:T(8,128)(2,1)}, bf16[256,1152]{1,0:T(8,128)(2,1)}, u32[]{:S(2)}, u32[]{:S(2)}) %collective-permute-start.1) | collective-permute-done | bytes 589856 | tf_op jit(solution)/shard_map/ppermute | solution.py:11
  260.8 0.0 collective-permute-done
  260.8 3.1 fusion
  263.9 4.4 %collective-permute-start.2 = (f32[256,1152]{1,0:T(8,128)}, f32[256,1152]{1,0:T(8,128)S(1)}, u32[]{:S(2)}, u32[]{:S(2)}) collective-permute-start(f32[256,1152]{1,0:T(8,128)} %fusion), channel_id=1, source_target_pairs={{0,64},{64,128},{128,192},{192,256},{256,320},{320,384},{384,448},... | collective-permute-start | bytes 3538952 | tf_op jit(solution)/shard_map/ppermute | solution.py:11
  268.3 1.9 collective-permute-start.3
  270.2 17.8 %collective-permute-done.3 = bf16[256,1152]{1,0:T(8,128)(2,1)} collective-permute-done((bf16[256,1152]{1,0:T(8,128)(2,1)}, bf16[256,1152]{1,0:T(8,128)(2,1)}, u32[]{:S(2)}, u32[]{:S(2)}) %collective-permute-start.3) | collective-permute-done | bytes 589856 | tf_op jit(solution)/shard_map/ppermute | solution.py:11
  288.0 0.0 collective-permute-done.2
  288.0 3.1 fusion.29
  291.1 4.4 %collective-permute-start.4 = (f32[256,1152]{1,0:T(8,128)}, f32[256,1152]{1,0:T(8,128)S(1)}, u32[]{:S(2)}, u32[]{:S(2)}) collective-permute-start(f32[256,1152]{1,0:T(8,128)} %fusion.29), channel_id=1, source_target_pairs={{0,64},{64,128},{128,192},{192,256},{256,320},{320,384},{384,448},... | collective-permute-start | bytes 3538952 | tf_op jit(solution)/shard_map/ppermute | solution.py:11
  295.5 1.9 collective-permute-start.5
  297.4 17.8 %collective-permute-done.5 = bf16[256,1152]{1,0:T(8,128)(2,1)} collective-permute-done((bf16[256,1152]{1,0:T(8,128)(2,1)}, bf16[256,1152]{1,0:T(8,128)(2,1)}, u32[]{:S(2)}, u32[]{:S(2)}) %collective-permute-start.5) | collective-permute-done | bytes 589856 | tf_op jit(solution)/shard_map/ppermute | solution.py:11
  315.3 0.0 collective-permute-done.4
  315.3 3.1 fusion.28
  318.3 6.6 %collective-permute-start.6 = (f32[256,1152]{1,0:T(8,128)}, f32[256,1152]{1,0:T(8,128)S(1)}, u32[]{:S(2)}, u32[]{:S(2)}) collective-permute-start(f32[256,1152]{1,0:T(8,128)} %fusion.28), channel_id=1, source_target_pairs={{0,832},{64,896},{128,960},{192,0},{256,64},{320,128},{384,192},{4... | collective-permute-start | bytes 3538952 | tf_op jit(solution)/shard_map/ppermute | solution.py:11
  325.0 48.8 %collective-permute-done.6 = f32[256,1152]{1,0:T(8,128)S(1)} collective-permute-done((f32[256,1152]{1,0:T(8,128)}, f32[256,1152]{1,0:T(8,128)S(1)}, u32[]{:S(2)}, u32[]{:S(2)}) %collective-permute-start.6) | collective-permute-done | bytes 1179680 | tf_op jit(solution)/shard_map/ppermute | solution.py:11
  373.7 0.3 multiply_reduce_fusion
  374.0 3.7 convolution_convert_fusion
  (2 shorter events, 0.0 us)
Async XLA Ops:
  6.5 221.8 %copy-start = (bf16[256,1152]{1,0:T(8,128)(2,1)S(1)}, bf16[256,1152]{1,0:T(8,128)(2,1)}, u32[]{:S(2)}) copy-start(bf16[256,1152]{1,0:T(8,128)(2,1)} %param.6) | copy-start | bytes 1769476
  6.5 216.4 %all-gather.3.cloned.1.call-start = ((), (), s32[]{:S(2)}) async-start(), calls=%async_computation | async-start | bytes 3594240 | tf_op jit(solution)/shard_map/all_gather | solution.py:21
  231.1 1.1 copy-start.1
  231.3 0.8 copy-start.2
  234.2 26.6 %collective-permute-start = (f32[256,1152]{1,0:T(8,128)}, f32[256,1152]{1,0:T(8,128)S(1)}, u32[]{:S(2)}, u32[]{:S(2)}) collective-permute-start(f32[256,1152]{1,0:T(8,128)} %convolution_multiply_fusion.3), channel_id=1, source_target_pairs={{0,64},{64,128},{128,192},{192,256},{256,320},{320,384},{384,448},... | collective-permute-start | bytes 3538952 | tf_op jit(solution)/shard_map/ppermute | solution.py:11
  241.0 19.8 %collective-permute-start.1 = (bf16[256,1152]{1,0:T(8,128)(2,1)}, bf16[256,1152]{1,0:T(8,128)(2,1)}, u32[]{:S(2)}, u32[]{:S(2)}) collective-permute-start(bf16[256,1152]{1,0:T(8,128)(2,1)} %copy-done.2), channel_id=1, source_target_pairs={{0,64},{64,128},{128,192},{192,256},{256,320},{320,384},{384,448},... | collective-permute-start | bytes 1769480 | tf_op jit(solution)/shard_map/ppermute | solution.py:11
  263.9 24.1 %collective-permute-start.2 = (f32[256,1152]{1,0:T(8,128)}, f32[256,1152]{1,0:T(8,128)S(1)}, u32[]{:S(2)}, u32[]{:S(2)}) collective-permute-start(f32[256,1152]{1,0:T(8,128)} %fusion), channel_id=1, source_target_pairs={{0,64},{64,128},{128,192},{192,256},{256,320},{320,384},{384,448},... | collective-permute-start | bytes 3538952 | tf_op jit(solution)/shard_map/ppermute | solution.py:11
  268.3 19.8 %collective-permute-start.3 = (bf16[256,1152]{1,0:T(8,128)(2,1)}, bf16[256,1152]{1,0:T(8,128)(2,1)}, u32[]{:S(2)}, u32[]{:S(2)}) collective-permute-start(bf16[256,1152]{1,0:T(8,128)(2,1)} %collective-permute-done.1), channel_id=1, source_target_pairs={{0,64},{64,128},{128,192},{192,256},{256,320},{320,384},{384,448},... | collective-permute-start | bytes 1769480 | tf_op jit(solution)/shard_map/ppermute | solution.py:11
  291.1 24.1 %collective-permute-start.4 = (f32[256,1152]{1,0:T(8,128)}, f32[256,1152]{1,0:T(8,128)S(1)}, u32[]{:S(2)}, u32[]{:S(2)}) collective-permute-start(f32[256,1152]{1,0:T(8,128)} %fusion.29), channel_id=1, source_target_pairs={{0,64},{64,128},{128,192},{192,256},{256,320},{320,384},{384,448},... | collective-permute-start | bytes 3538952 | tf_op jit(solution)/shard_map/ppermute | solution.py:11
  295.5 19.8 %collective-permute-start.5 = (bf16[256,1152]{1,0:T(8,128)(2,1)}, bf16[256,1152]{1,0:T(8,128)(2,1)}, u32[]{:S(2)}, u32[]{:S(2)}) collective-permute-start(bf16[256,1152]{1,0:T(8,128)(2,1)} %collective-permute-done.3), channel_id=1, source_target_pairs={{0,64},{64,128},{128,192},{192,256},{256,320},{320,384},{384,448},... | collective-permute-start | bytes 1769480 | tf_op jit(solution)/shard_map/ppermute | solution.py:11
  318.3 55.4 %collective-permute-start.6 = (f32[256,1152]{1,0:T(8,128)}, f32[256,1152]{1,0:T(8,128)S(1)}, u32[]{:S(2)}, u32[]{:S(2)}) collective-permute-start(f32[256,1152]{1,0:T(8,128)} %fusion.28), channel_id=1, source_target_pairs={{0,832},{64,896},{128,960},{192,0},{256,64},{320,128},{384,192},{4... | collective-permute-start | bytes 3538952 | tf_op jit(solution)/shard_map/ppermute | solution.py:11
Sparse Core Ops, SparseCore 0:
  13.2 209.7 all-gather.2
where the time goes:
time: 385 us
  waiting for transfers between devices  316 us (82%)
  starting transfers between devices  27.9 us (7%)
  matrix products  17.8 us (5%)
  between operations  14.8 us (4%)
  local copies, waits for them, and re-layouts  6.29 us (2%)
    all_gather x1, waiting for transfers between devices, body(): full_proj = lax.all_gather(text_proj, 'dev', axis=0, tiled=True)  213 us
    ppermute x7, waiting for transfers between devices, passed_along(): lax.ppermute(value, axis, [(i, (i + by) % count) for i in range(count)])  102 us
    ppermute x7, starting transfers between devices, passed_along(): lax.ppermute(value, axis, [(i, (i + by) % count) for i in range(count)])  27.9 us
    dot_general x4, matrix products, body(): jnp.dot(weights, unit_img, preferred_element_type=jnp.float32)  11.3 us
  transfers between devices with their start and end apart: 8, of which 5 were waited for; matrix products, arithmetic and copies ran while one was open for 0% of the time, Pallas kernels for 0%

commit v1 on v0

v1 whole, which is shorter than its diff:
```python
import jax
import jax.numpy as jnp
from jax import lax
from jax.experimental import pallas as pl
from jax.experimental.pallas import tpu as pltpu
from jax.sharding import PartitionSpec as P

norm_eps = 1e-06
AXES = ("island", "dev")
NX, NY, NZH = 4, 8, 2


def coords(i, n_dev):
    isl, dev = divmod(i, n_dev)
    return isl, dev // (NY * NZH), dev // NZH % NY, dev % NZH


def moved(value, to):
    n_isl, n_dev = lax.axis_size("island"), lax.axis_size("dev")
    pairs = []
    for i in range(n_isl * n_dev):
        target = to(*coords(i, n_dev))
        if target is not None:
            isl, x, y, zh = target
            pairs.append(
                (i, (isl % n_isl) * n_dev + ((x % NX) * NY + y % NY) * NZH + zh % NZH)
            )
    return lax.ppermute(value, AXES, pairs)


def tail_kernel(
    idx, scal, im0, im1, im2, im3, text,
    m0, mm, m2, mp, o0, om, o2, op,
    out_ref,
    raw, unit, txt, sets, full, hid, sems,
):
    x, y, c = idx[0], idx[1], idx[2]
    rows = out_ref.shape[0]
    copies = []
    for k, src in enumerate((im0, im1, im2, im3)):
        copies.append(pltpu.make_async_copy(src, raw.at[pl.ds(k * rows, rows)], sems.at[k]))
    copies.append(pltpu.make_async_copy(text, txt, sems.at[4]))
    k = 5
    for core, group in ((c, (m0, mp, m2, mm)), (1 - c, (o0, op, o2, om))):
        for rel, src in enumerate(group):
            slot = core * NX + lax.rem(x + rel, NX)
            copies.append(pltpu.make_async_copy(src, sets.at[slot], sems.at[k]))
            k += 1
    for copy in copies:
        copy.start()

    for k in range(4):
        copies[k].wait()
        f = raw[pl.ds(k * rows, rows), :].astype(jnp.float32)
        s = lax.rsqrt(jnp.sum(f * f, axis=1, keepdims=True) + norm_eps)
        unit[pl.ds(k * rows, rows), :] = (f * s).astype(jnp.bfloat16)

    for copy in copies[4:]:
        copy.wait()

    for xx in range(NX):
        for half in range(2):
            slabs = []
            for yy in range(half * 4, half * 4 + 4):
                j = lax.rem(y - yy + NY, NY)
                far = (j >= 4).astype(jnp.int32)
                pos = jnp.where(j < 4, j, 7 - j)
                slabs.append(sets[far * NX + xx, pos].astype(jnp.float32))
            block = jnp.concatenate(slabs, axis=0).astype(jnp.bfloat16)
            full[pl.ds(xx * 288 + half * 144, 144), :] = block

    hidden = jnp.dot(txt[...], full[...], preferred_element_type=jnp.float32)
    inv = lax.rsqrt(jnp.sum(hidden * hidden, axis=1, keepdims=True) + norm_eps)
    hid[...] = hidden * inv
    text_b = hid[...].astype(jnp.bfloat16)
    scale, bias = scal[0], scal[1]
    grad = jnp.zeros(hid.shape, jnp.float32)
    for t in range(4):
        u = unit[pl.ds(t * rows, rows), :]
        scores = scale * lax.dot_general(
            text_b, u, (((1,), (1,)), ((), ())), preferred_element_type=jnp.float32
        ) + bias
        probs = jax.nn.sigmoid(scores)
        if t == 0:
            r = lax.broadcasted_iota(jnp.int32, (rows, rows), 0)
            s = lax.broadcasted_iota(jnp.int32, (rows, rows), 1)
            probs = probs - (r == s).astype(jnp.float32)
        grad = grad + jnp.dot(
            probs.astype(jnp.bfloat16), u, preferred_element_type=jnp.float32
        )
    grad = grad * scale
    unit_txt = hid[...]
    radial = jnp.sum(unit_txt * grad, axis=1, keepdims=True)
    grad_hidden = ((grad - unit_txt * radial) * inv).astype(jnp.bfloat16)
    out_ref[...] = lax.dot_general(
        grad_hidden, full[...], (((1,), (1,)), ((), ())), preferred_element_type=jnp.float32
    ).astype(jnp.bfloat16)


def body(image_embed, text_feat, text_proj, log_scale, bias):
    rows, width = text_feat.shape
    isl = lax.axis_index("island").astype(jnp.int32)
    dev = lax.axis_index("dev").astype(jnp.int32)
    c, x, y, zh = isl % 2, dev // (NY * NZH), dev // NZH % NY, dev % NZH

    far = moved(text_proj, lambda i, x, y, z: (i, x, y - i % 2, 1 - z))
    near = moved(text_proj, lambda i, x, y, z: (i, x, y - 1, z) if i % 2 else None)
    base = jnp.where(c == 0, text_proj, near)
    pair = jnp.where(
        zh == 0, jnp.concatenate([base, far]), jnp.concatenate([far, base])
    )

    two = moved(image_embed, lambda i, x, y, z: (i - 2, x, y, z))
    chip = moved(image_embed, lambda i, x, y, z: (i ^ 1, x, y, z))

    got = [
        moved(pair, lambda i, x, y, z, k=k: (i, x, y + (-k if i % 2 else k), z))
        for k in (1, 2, 3)
    ]
    mine = jnp.stack([pair] + got)
    minus = moved(mine, lambda i, x, y, z: (i, x + 1, y, z))
    plus = moved(mine, lambda i, x, y, z: (i, x - 1, y, z))
    o0 = moved(mine, lambda i, x, y, z: (i ^ 1, x, y, z))
    swapped = moved(two, lambda i, x, y, z: (i ^ 1, x, y, z))
    ahead = moved(two, lambda i, x, y, z: (i - 1, x, y, z) if i % 2 == 0 else None)

    across = moved(
        jnp.where(c == 0, minus, plus), lambda i, x, y, z: (i, x + (-1 if i % 2 else 1), y, z)
    )
    om = moved(minus, lambda i, x, y, z: (i ^ 1, x, y, z))
    op = moved(plus, lambda i, x, y, z: (i ^ 1, x, y, z))
    o2 = moved(across, lambda i, x, y, z: (i ^ 1, x, y, z))

    im1 = jnp.where(c == 0, chip, ahead)
    idx = jnp.stack([x, y, c])
    scal = jnp.stack([jnp.exp(log_scale), bias])
    any_spec = pl.BlockSpec(memory_space=pl.ANY)
    smem = pl.BlockSpec(memory_space=pltpu.SMEM)
    return pl.pallas_call(
        tail_kernel,
        out_shape=jax.ShapeDtypeStruct((rows, width), jnp.bfloat16),
        in_specs=[smem, smem] + [any_spec] * 13,
        out_specs=pl.BlockSpec(memory_space=pltpu.VMEM),
        scratch_shapes=[
            pltpu.VMEM((4 * rows, width), jnp.bfloat16),
            pltpu.VMEM((4 * rows, width), jnp.bfloat16),
            pltpu.VMEM((rows, width), jnp.bfloat16),
            pltpu.VMEM((2 * NX, 4, 36, width), jnp.bfloat16),
            pltpu.VMEM((width, width), jnp.bfloat16),
            pltpu.VMEM((rows, width), jnp.float32),
            pltpu.SemaphoreType.DMA((13,)),
        ],
        compiler_params=pltpu.CompilerParams(vmem_limit_bytes=48 * 1024 * 1024),
        cost_estimate=pl.CostEstimate(
            flops=2 * 2 * rows * width * (width + 4 * rows),
            bytes_accessed=8 * 1024 * 1024,
            transcendentals=4 * rows * rows,
        ),
    )(
        idx, scal, image_embed, im1, two, swapped, text_feat,
        mine, minus, across, plus, o0, om, o2, op,
    )


def solution(mesh):
    placed = (P(AXES, None), P(AXES, None), P("dev", None), P(), P())
    return jax.shard_map(
        body, mesh=mesh, in_specs=placed, out_specs=P(AXES, None), check_vma=False
    )
```

time: 385 us -> 94.7 us (0.25)
  the two profiles are of different devices: /device:TPU:1 before, /device:TPU:9 now
where the time goes in v1:
time: 94.7 us; the launch traced here: 94.1 us
  starting transfers between devices  64.9 us (69%)
  waiting for transfers between devices  16.5 us (17%)
  Pallas kernels  8.78 us (9%)
  other arithmetic  2.26 us (2%)
  between operations  1.66 us (2%)
    ppermute x16, starting transfers between devices, moved(): return lax.ppermute(value, AXES, pairs)  64.9 us
    ppermute x16, waiting for transfers between devices, moved(): return lax.ppermute(value, AXES, pairs)  16.5 us
    pallas_call x1, Pallas kernels, body(): pl.pallas_call(tail_kernel, out_shape=jax.ShapeDtypeStruct((rows, width),...  8.78 us
  transfers between devices with their start and end apart: 16, of which 5 were waited for; matrix products, arithmetic and copies ran while one was open for 2% of the time, Pallas kernels for 0%

profile of v1, /device:TPU:9, one launch (start us, length us, event | category | flops | bytes accessed | tf_op | source)
XLA Modules:
  0.0 94.1 jit_solution(3779460756449782369)
XLA Ops:
  0.0 0.0 copy-start.2
  0.0 2.0 %collective-permute-start.4 = (bf16[18,1152]{1,0:T(8,128)(2,1)}, bf16[18,1152]{1,0:T(8,128)(2,1)S(1)}, u32[]{:S(2)}, u32[]{:S(2)}) collective-permute-start(bf16[18,1152]{1,0:T(8,128)(2,1)} %param.7), channel_id=1, source_target_pairs={{64,78},{65,79},{66,64},{67,65},{68,66},{69,67},{70,68},{71,69},{7... | collective-permute-start | bytes 124424 | tf_op jit(solution)/shard_map/ppermute | solution.py:28
  2.0 22.1 %collective-permute-start.5 = (bf16[18,1152]{1,0:T(8,128)(2,1)}, bf16[18,1152]{1,0:T(8,128)(2,1)S(1)}, u32[]{:S(2)}, u32[]{:S(2)}) collective-permute-start(bf16[18,1152]{1,0:T(8,128)(2,1)} %param.7), channel_id=1, source_target_pairs={{0,1},{1,0},{2,3},{3,2},{4,5},{5,4},{6,7},{7,6},{8,9},{9,8},{10,11... | collective-permute-start | bytes 124424 | tf_op jit(solution)/shard_map/ppermute | solution.py:28
  24.2 8.6 %collective-permute-start.1 = (bf16[256,1152]{1,0:T(8,128)(2,1)}, bf16[256,1152]{1,0:T(8,128)(2,1)S(1)}, u32[]{:S(2)}, u32[]{:S(2)}) collective-permute-start(bf16[256,1152]{1,0:T(8,128)(2,1)} %im0.1), channel_id=1, source_target_pairs={{0,896},{1,897},{2,898},{3,899},{4,900},{5,901},{6,902},{7,903},{8... | collective-permute-start | bytes 1769480 | tf_op jit(solution)/shard_map/ppermute | solution.py:28
  32.8 0.0 collective-permute-done.4
  32.8 0.0 copy-done.2
  32.8 0.0 copy-start
  32.8 0.0 collective-permute-done.5
  32.9 3.1 %collective-permute-start.6 = (bf16[36,1152]{1,0:T(8,128)(2,1)S(1)}, bf16[36,1152]{1,0:T(8,128)(2,1)S(1)}, u32[]{:S(2)}, u32[]{:S(2)}) collective-permute-start(bf16[36,1152]{1,0:T(8,128)(2,1)S(1)} %maximum_select_fusion.1), channel_id=1, source_target_pairs={{0,2},{1,3},{2,4},{3,5},{4,6},{5,7},{6,8},{7,9},{8,10},{9,11},{10,... | collective-permute-start | bytes 248840 | tf_op jit(solution)/shard_map/ppermute | solution.py:28
  36.0 3.8 %collective-permute-start.7 = (bf16[36,1152]{1,0:T(8,128)(2,1)S(1)}, bf16[36,1152]{1,0:T(8,128)(2,1)S(1)}, u32[]{:S(2)}, u32[]{:S(2)}) collective-permute-start(bf16[36,1152]{1,0:T(8,128)(2,1)S(1)} %maximum_select_fusion.1), channel_id=1, source_target_pairs={{0,4},{1,5},{2,6},{3,7},{4,8},{5,9},{6,10},{7,11},{8,12},{9,13},{1... | collective-permute-start | bytes 248840 | tf_op jit(solution)/shard_map/ppermute | solution.py:28
  39.8 1.9 %collective-permute-start.8 = (bf16[36,1152]{1,0:T(8,128)(2,1)S(1)}, bf16[36,1152]{1,0:T(8,128)(2,1)S(1)}, u32[]{:S(2)}, u32[]{:S(2)}) collective-permute-start(bf16[36,1152]{1,0:T(8,128)(2,1)S(1)} %maximum_select_fusion.1), channel_id=1, source_target_pairs={{0,6},{1,7},{2,8},{3,9},{4,10},{5,11},{6,12},{7,13},{8,14},{9,15},... | collective-permute-start | bytes 248840 | tf_op jit(solution)/shard_map/ppermute | solution.py:28
  41.8 0.0 collective-permute-done.6
  41.8 0.5 collective-permute-done.7
  42.3 7.3 %collective-permute-done.8 = bf16[36,1152]{1,0:T(8,128)(2,1)S(1)} collective-permute-done((bf16[36,1152]{1,0:T(8,128)(2,1)S(1)}, bf16[36,1152]{1,0:T(8,128)(2,1)S(1)}, u32[]{:S(2)}, u32[]{:S(2)}) %collective-permute-start.8) | collective-permute-done | bytes 82976 | tf_op jit(solution)/shard_map/ppermute | solution.py:28
  49.7 0.1 pad_maximum_fusion.m0
  49.7 4.4 %collective-permute-start.10 = (bf16[4,36,1152]{2,1,0:T(8,128)(2,1)S(1)}, bf16[4,36,1152]{2,1,0:T(8,128)(2,1)S(1)}, u32[]{:S(2)}, u32[]{:S(2)}) collective-permute-start(bf16[4,36,1152]{2,1,0:T(8,128)(2,1)S(1)} %pad_maximum_fusion.m0), channel_id=1, source_target_pairs={{0,48},{1,49},{2,50},{3,51},{4,52},{5,53},{6,54},{7,55},{8,56},{9,... | collective-permute-start | bytes 995336 | tf_op jit(solution)/shard_map/ppermute | solution.py:28
  54.1 1.9 %collective-permute-start.9 = (bf16[4,36,1152]{2,1,0:T(8,128)(2,1)S(1)}, bf16[4,36,1152]{2,1,0:T(8,128)(2,1)S(1)}, u32[]{:S(2)}, u32[]{:S(2)}) collective-permute-start(bf16[4,36,1152]{2,1,0:T(8,128)(2,1)S(1)} %pad_maximum_fusion.m0), channel_id=1, source_target_pairs={{0,16},{1,17},{2,18},{3,19},{4,20},{5,21},{6,22},{7,23},{8,24},{9,... | collective-permute-start | bytes 995336 | tf_op jit(solution)/shard_map/ppermute | solution.py:28
  56.1 0.0 copy-done
  56.1 1.9 %collective-permute-start = (bf16[256,1152]{1,0:T(8,128)(2,1)S(1)}, bf16[256,1152]{1,0:T(8,128)(2,1)S(1)}, u32[]{:S(2)}, u32[]{:S(2)}) collective-permute-start(bf16[256,1152]{1,0:T(8,128)(2,1)S(1)} %copy-done), channel_id=1, source_target_pairs={{0,64},{1,65},{2,66},{3,67},{4,68},{5,69},{6,70},{7,71},{8,72},{9,... | collective-permute-start | bytes 1769480 | tf_op jit(solution)/shard_map/ppermute | solution.py:28
  58.0 0.0 collective-permute-done.1.im2
  58.0 1.3 %collective-permute-start.2 = (bf16[256,1152]{1,0:T(8,128)(2,1)S(1)}, bf16[256,1152]{1,0:T(8,128)(2,1)}, u32[]{:S(2)}, u32[]{:S(2)}) collective-permute-start(bf16[256,1152]{1,0:T(8,128)(2,1)S(1)} %collective-permute-done.1.im2), channel_id=1, source_target_pairs={{0,960},{1,961},{2,962},{3,963},{4,964},{5,965},{6,966},{7,967},{8... | collective-permute-start | bytes 1769480 | tf_op jit(solution)/shard_map/ppermute | solution.py:28
  59.3 3.0 %collective-permute-done.10.mp = bf16[4,36,1152]{2,1,0:T(8,128)(2,1)S(1)} collective-permute-done((bf16[4,36,1152]{2,1,0:T(8,128)(2,1)S(1)}, bf16[4,36,1152]{2,1,0:T(8,128)(2,1)S(1)}, u32[]{:S(2)}, u32[]{:S(2)}) %collective-permute-start.10) | collective-permute-done | bytes 331808 | tf_op jit(solution)/shard_map/ppermute | solution.py:28
  62.3 5.1 %collective-permute-done.9.mm = bf16[4,36,1152]{2,1,0:T(8,128)(2,1)S(1)} collective-permute-done((bf16[4,36,1152]{2,1,0:T(8,128)(2,1)S(1)}, bf16[4,36,1152]{2,1,0:T(8,128)(2,1)S(1)}, u32[]{:S(2)}, u32[]{:S(2)}) %collective-permute-start.9) | collective-permute-done | bytes 331808 | tf_op jit(solution)/shard_map/ppermute | solution.py:28
  67.4 0.8 broadcast_select_fusion.1
  68.2 1.9 %collective-permute-start.11 = (bf16[4,36,1152]{2,1,0:T(8,128)(2,1)}, bf16[4,36,1152]{2,1,0:T(8,128)(2,1)S(1)}, u32[]{:S(2)}, u32[]{:S(2)}) collective-permute-start(bf16[4,36,1152]{2,1,0:T(8,128)(2,1)} %broadcast_select_fusion.1), channel_id=1, source_target_pairs={{0,16},{1,17},{2,18},{3,19},{4,20},{5,21},{6,22},{7,23},{8,24},{9,... | collective-permute-start | bytes 995336 | tf_op jit(solution)/shard_map/ppermute | solution.py:28
  71.5 0.1 pad_maximum_fusion.1.scal
  71.6 2.7 %collective-permute-start.3 = (bf16[256,1152]{1,0:T(8,128)(2,1)S(1)}, bf16[256,1152]{1,0:T(8,128)(2,1)S(1)}, u32[]{:S(2)}, u32[]{:S(2)}) collective-permute-start(bf16[256,1152]{1,0:T(8,128)(2,1)S(1)} %collective-permute-done.1.im2), channel_id=1, source_target_pairs={{0,64},{1,65},{2,66},{3,67},{4,68},{5,69},{6,70},{7,71},{8,72},{9,... | collective-permute-start | bytes 1769480 | tf_op jit(solution)/shard_map/ppermute | solution.py:28
  74.3 0.1 pad_add_fusion.idx
  74.4 0.0 copy-start.1
  74.4 2.0 %collective-permute-start.12 = (bf16[4,36,1152]{2,1,0:T(8,128)(2,1)S(1)}, bf16[4,36,1152]{2,1,0:T(8,128)(2,1)S(1)}, u32[]{:S(2)}, u32[]{:S(2)}) collective-permute-start(bf16[4,36,1152]{2,1,0:T(8,128)(2,1)S(1)} %pad_maximum_fusion.m0), channel_id=1, source_target_pairs={{0,64},{1,65},{2,66},{3,67},{4,68},{5,69},{6,70},{7,71},{8,72},{9,... | collective-permute-start | bytes 995336 | tf_op jit(solution)/shard_map/ppermute | solution.py:28
  76.4 0.0 collective-permute-done
  76.4 2.4 %collective-permute-start.13 = (bf16[4,36,1152]{2,1,0:T(8,128)(2,1)S(1)}, bf16[4,36,1152]{2,1,0:T(8,128)(2,1)S(1)}, u32[]{:S(2)}, u32[]{:S(2)}) collective-permute-start(bf16[4,36,1152]{2,1,0:T(8,128)(2,1)S(1)} %collective-permute-done.9.mm), channel_id=1, source_target_pairs={{0,64},{1,65},{2,66},{3,67},{4,68},{5,69},{6,70},{7,71},{8,72},{9,... | collective-permute-start | bytes 995336 | tf_op jit(solution)/shard_map/ppermute | solution.py:28
  78.9 0.0 collective-permute-done.11.m2
  78.9 2.9 %collective-permute-start.15 = (bf16[4,36,1152]{2,1,0:T(8,128)(2,1)S(1)}, bf16[4,36,1152]{2,1,0:T(8,128)(2,1)S(1)}, u32[]{:S(2)}, u32[]{:S(2)}) collective-permute-start(bf16[4,36,1152]{2,1,0:T(8,128)(2,1)S(1)} %collective-permute-done.10.mp), channel_id=1, source_target_pairs={{0,64},{1,65},{2,66},{3,67},{4,68},{5,69},{6,70},{7,71},{8,72},{9,... | collective-permute-start | bytes 995336 | tf_op jit(solution)/shard_map/ppermute | solution.py:28
  81.8 0.0 collective-permute-done.2
  81.8 1.9 %collective-permute-start.14 = (bf16[4,36,1152]{2,1,0:T(8,128)(2,1)S(1)}, bf16[4,36,1152]{2,1,0:T(8,128)(2,1)S(1)}, u32[]{:S(2)}, u32[]{:S(2)}) collective-permute-start(bf16[4,36,1152]{2,1,0:T(8,128)(2,1)S(1)} %collective-permute-done.11.m2), channel_id=1, source_target_pairs={{0,64},{1,65},{2,66},{3,67},{4,68},{5,69},{6,70},{7,71},{8,72},{9,... | collective-permute-start | bytes 995336 | tf_op jit(solution)/shard_map/ppermute | solution.py:28
  83.7 1.1 %broadcast_select_fusion.im1 = bf16[256,1152]{1,0:T(8,128)(2,1)S(1)} fusion(bf16[256,1152]{1,0:T(8,128)(2,1)S(1)} %collective-permute-done, bf16[256,1152]{1,0:T(8,128)(2,1)} %collective-permute-done.2, pred[]{:T(512)S(6)} %eq.12), kind=kLoop, calls=%fused_computation | loop fusion | flops 294912 | bytes 1769473 | tf_op jit(solution)/shard_map/jit(_where)/select_n | solution.py:134
  84.8 0.0 collective-permute-done.12.o0
  84.8 0.0 collective-permute-done.13.om
  84.9 0.0 collective-permute-done.15.op
  84.9 0.5 collective-permute-done.14.o2
  85.3 0.0 collective-permute-done.3.im3
  85.3 0.0 copy-done.1
  85.4 8.8 %shard_map.55 = bf16[256,1152]{1,0:T(8,128)(2,1)} custom-call(s32[3]{0:T(128)S(1)} %pad_add_fusion.idx, f32[2]{0:T(128)S(1)} %pad_maximum_fusion.1.scal, bf16[256,1152]{1,0:T(8,128)(2,1)S(1)} %copy-done, bf16[256,1152]{1,0:T(8,128)(2,1)S(1)} %broadcast_select_fusion.im1, bf16[256,1152]{1,0:T(8,128)(2,1)S(1)} %collective-permute-done.1.im2, ...), custom_call_target="tpu_custom_call" | custom-call | flops 2566914048 | bytes 8388608 | tf_op jit(solution)/shard_map/pallas_call | solution.py:139
  (3 shorter events, 0.1 us)
Async XLA Ops:
  0.0 32.8 %copy-start.2 = (bf16[18,1152]{1,0:T(8,128)(2,1)S(1)}, bf16[18,1152]{1,0:T(8,128)(2,1)}, u32[]{:S(2)}) copy-start(bf16[18,1152]{1,0:T(8,128)(2,1)} %param.7) | copy-start | bytes 124420
  0.0 32.8 %collective-permute-start.4 = (bf16[18,1152]{1,0:T(8,128)(2,1)}, bf16[18,1152]{1,0:T(8,128)(2,1)S(1)}, u32[]{:S(2)}, u32[]{:S(2)}) collective-permute-start(bf16[18,1152]{1,0:T(8,128)(2,1)} %param.7), channel_id=1, source_target_pairs={{64,78},{65,79},{66,64},{67,65},{68,66},{69,67},{70,68},{71,69},{7... | collective-permute-start | bytes 124424 | tf_op jit(solution)/shard_map/ppermute | solution.py:28
  2.0 30.8 %collective-permute-start.5 = (bf16[18,1152]{1,0:T(8,128)(2,1)}, bf16[18,1152]{1,0:T(8,128)(2,1)S(1)}, u32[]{:S(2)}, u32[]{:S(2)}) collective-permute-start(bf16[18,1152]{1,0:T(8,128)(2,1)} %param.7), channel_id=1, source_target_pairs={{0,1},{1,0},{2,3},{3,2},{4,5},{5,4},{6,7},{7,6},{8,9},{9,8},{10,11... | collective-permute-start | bytes 124424 | tf_op jit(solution)/shard_map/ppermute | solution.py:28
  24.2 33.8 %collective-permute-start.1 = (bf16[256,1152]{1,0:T(8,128)(2,1)}, bf16[256,1152]{1,0:T(8,128)(2,1)S(1)}, u32[]{:S(2)}, u32[]{:S(2)}) collective-permute-start(bf16[256,1152]{1,0:T(8,128)(2,1)} %im0.1), channel_id=1, source_target_pairs={{0,896},{1,897},{2,898},{3,899},{4,900},{5,901},{6,902},{7,903},{8... | collective-permute-start | bytes 1769480 | tf_op jit(solution)/shard_map/ppermute | solution.py:28
  32.8 23.2 %copy-start = (bf16[256,1152]{1,0:T(8,128)(2,1)S(1)}, bf16[256,1152]{1,0:T(8,128)(2,1)}, u32[]{:S(2)}) copy-start(bf16[256,1152]{1,0:T(8,128)(2,1)} %im0.1) | copy-start | bytes 1769476
  32.9 8.9 %collective-permute-start.6 = (bf16[36,1152]{1,0:T(8,128)(2,1)S(1)}, bf16[36,1152]{1,0:T(8,128)(2,1)S(1)}, u32[]{:S(2)}, u32[]{:S(2)}) collective-permute-start(bf16[36,1152]{1,0:T(8,128)(2,1)S(1)} %maximum_select_fusion.1), channel_id=1, source_target_pairs={{0,2},{1,3},{2,4},{3,5},{4,6},{5,7},{6,8},{7,9},{8,10},{9,11},{10,... | collective-permute-start | bytes 248840 | tf_op jit(solution)/shard_map/ppermute | solution.py:28
  36.0 6.3 %collective-permute-start.7 = (bf16[36,1152]{1,0:T(8,128)(2,1)S(1)}, bf16[36,1152]{1,0:T(8,128)(2,1)S(1)}, u32[]{:S(2)}, u32[]{:S(2)}) collective-permute-start(bf16[36,1152]{1,0:T(8,128)(2,1)S(1)} %maximum_select_fusion.1), channel_id=1, source_target_pairs={{0,4},{1,5},{2,6},{3,7},{4,8},{5,9},{6,10},{7,11},{8,12},{9,13},{1... | collective-permute-start | bytes 248840 | tf_op jit(solution)/shard_map/ppermute | solution.py:28
  39.8 9.9 %collective-permute-start.8 = (bf16[36,1152]{1,0:T(8,128)(2,1)S(1)}, bf16[36,1152]{1,0:T(8,128)(2,1)S(1)}, u32[]{:S(2)}, u32[]{:S(2)}) collective-permute-start(bf16[36,1152]{1,0:T(8,128)(2,1)S(1)} %maximum_select_fusion.1), channel_id=1, source_target_pairs={{0,6},{1,7},{2,8},{3,9},{4,10},{5,11},{6,12},{7,13},{8,14},{9,15},... | collective-permute-start | bytes 248840 | tf_op jit(solution)/shard_map/ppermute | solution.py:28
  49.7 12.6 %collective-permute-start.10 = (bf16[4,36,1152]{2,1,0:T(8,128)(2,1)S(1)}, bf16[4,36,1152]{2,1,0:T(8,128)(2,1)S(1)}, u32[]{:S(2)}, u32[]{:S(2)}) collective-permute-start(bf16[4,36,1152]{2,1,0:T(8,128)(2,1)S(1)} %pad_maximum_fusion.m0), channel_id=1, source_target_pairs={{0,48},{1,49},{2,50},{3,51},{4,52},{5,53},{6,54},{7,55},{8,56},{9,... | collective-permute-start | bytes 995336 | tf_op jit(solution)/shard_map/ppermute | solution.py:28
  54.1 13.3 %collective-permute-start.9 = (bf16[4,36,1152]{2,1,0:T(8,128)(2,1)S(1)}, bf16[4,36,1152]{2,1,0:T(8,128)(2,1)S(1)}, u32[]{:S(2)}, u32[]{:S(2)}) collective-permute-start(bf16[4,36,1152]{2,1,0:T(8,128)(2,1)S(1)} %pad_maximum_fusion.m0), channel_id=1, source_target_pairs={{0,16},{1,17},{2,18},{3,19},{4,20},{5,21},{6,22},{7,23},{8,24},{9,... | collective-permute-start | bytes 995336 | tf_op jit(solution)/shard_map/ppermute | solution.py:28
  56.1 20.4 %collective-permute-start = (bf16[256,1152]{1,0:T(8,128)(2,1)S(1)}, bf16[256,1152]{1,0:T(8,128)(2,1)S(1)}, u32[]{:S(2)}, u32[]{:S(2)}) collective-permute-start(bf16[256,1152]{1,0:T(8,128)(2,1)S(1)} %copy-done), channel_id=1, source_target_pairs={{0,64},{1,65},{2,66},{3,67},{4,68},{5,69},{6,70},{7,71},{8,72},{9,... | collective-permute-start | bytes 1769480 | tf_op jit(solution)/shard_map/ppermute | solution.py:28
  58.0 23.7 %collective-permute-start.2 = (bf16[256,1152]{1,0:T(8,128)(2,1)S(1)}, bf16[256,1152]{1,0:T(8,128)(2,1)}, u32[]{:S(2)}, u32[]{:S(2)}) collective-permute-start(bf16[256,1152]{1,0:T(8,128)(2,1)S(1)} %collective-permute-done.1.im2), channel_id=1, source_target_pairs={{0,960},{1,961},{2,962},{3,963},{4,964},{5,965},{6,966},{7,967},{8... | collective-permute-start | bytes 1769480 | tf_op jit(solution)/shard_map/ppermute | solution.py:28
  68.2 10.6 %collective-permute-start.11 = (bf16[4,36,1152]{2,1,0:T(8,128)(2,1)}, bf16[4,36,1152]{2,1,0:T(8,128)(2,1)S(1)}, u32[]{:S(2)}, u32[]{:S(2)}) collective-permute-start(bf16[4,36,1152]{2,1,0:T(8,128)(2,1)} %broadcast_select_fusion.1), channel_id=1, source_target_pairs={{0,16},{1,17},{2,18},{3,19},{4,20},{5,21},{6,22},{7,23},{8,24},{9,... | collective-permute-start | bytes 995336 | tf_op jit(solution)/shard_map/ppermute | solution.py:28
  71.6 13.8 %collective-permute-start.3 = (bf16[256,1152]{1,0:T(8,128)(2,1)S(1)}, bf16[256,1152]{1,0:T(8,128)(2,1)S(1)}, u32[]{:S(2)}, u32[]{:S(2)}) collective-permute-start(bf16[256,1152]{1,0:T(8,128)(2,1)S(1)} %collective-permute-done.1.im2), channel_id=1, source_target_pairs={{0,64},{1,65},{2,66},{3,67},{4,68},{5,69},{6,70},{7,71},{8,72},{9,... | collective-permute-start | bytes 1769480 | tf_op jit(solution)/shard_map/ppermute | solution.py:28
  74.4 11.0 %copy-start.1 = (bf16[256,1152]{1,0:T(8,128)(2,1)S(1)}, bf16[256,1152]{1,0:T(8,128)(2,1)}, u32[]{:S(2)}) copy-start(bf16[256,1152]{1,0:T(8,128)(2,1)} %text.1) | copy-start | bytes 1769476
  74.4 10.5 %collective-permute-start.12 = (bf16[4,36,1152]{2,1,0:T(8,128)(2,1)S(1)}, bf16[4,36,1152]{2,1,0:T(8,128)(2,1)S(1)}, u32[]{:S(2)}, u32[]{:S(2)}) collective-permute-start(bf16[4,36,1152]{2,1,0:T(8,128)(2,1)S(1)} %pad_maximum_fusion.m0), channel_id=1, source_target_pairs={{0,64},{1,65},{2,66},{3,67},{4,68},{5,69},{6,70},{7,71},{8,72},{9,... | collective-permute-start | bytes 995336 | tf_op jit(solution)/shard_map/ppermute | solution.py:28
  76.4 8.4 %collective-permute-start.13 = (bf16[4,36,1152]{2,1,0:T(8,128)(2,1)S(1)}, bf16[4,36,1152]{2,1,0:T(8,128)(2,1)S(1)}, u32[]{:S(2)}, u32[]{:S(2)}) collective-permute-start(bf16[4,36,1152]{2,1,0:T(8,128)(2,1)S(1)} %collective-permute-done.9.mm), channel_id=1, source_target_pairs={{0,64},{1,65},{2,66},{3,67},{4,68},{5,69},{6,70},{7,71},{8,72},{9,... | collective-permute-start | bytes 995336 | tf_op jit(solution)/shard_map/ppermute | solution.py:28
  78.9 6.0 %collective-permute-start.15 = (bf16[4,36,1152]{2,1,0:T(8,128)(2,1)S(1)}, bf16[4,36,1152]{2,1,0:T(8,128)(2,1)S(1)}, u32[]{:S(2)}, u32[]{:S(2)}) collective-permute-start(bf16[4,36,1152]{2,1,0:T(8,128)(2,1)S(1)} %collective-permute-done.10.mp), channel_id=1, source_target_pairs={{0,64},{1,65},{2,66},{3,67},{4,68},{5,69},{6,70},{7,71},{8,72},{9,... | collective-permute-start | bytes 995336 | tf_op jit(solution)/shard_map/ppermute | solution.py:28
  81.8 3.6 %collective-permute-start.14 = (bf16[4,36,1152]{2,1,0:T(8,128)(2,1)S(1)}, bf16[4,36,1152]{2,1,0:T(8,128)(2,1)S(1)}, u32[]{:S(2)}, u32[]{:S(2)}) collective-permute-start(bf16[4,36,1152]{2,1,0:T(8,128)(2,1)S(1)} %collective-permute-done.11.m2), channel_id=1, source_target_pairs={{0,64},{1,65},{2,66},{3,67},{4,68},{5,69},{6,70},{7,71},{8,72},{9,... | collective-permute-start | bytes 995336 | tf_op jit(solution)/shard_map/ppermute | solution.py:28

commit v2 on v1

v2 whole, which is shorter than its diff:
```python
import jax
import jax.numpy as jnp
from jax import lax
from jax.experimental import pallas as pl
from jax.experimental.pallas import tpu as pltpu
from jax.sharding import PartitionSpec as P

norm_eps = 1e-06
AXES = ("island", "dev")
NX, NY, NZH = 4, 8, 2


def coords(i, n_dev):
    isl, dev = divmod(i, n_dev)
    return isl, dev // (NY * NZH), dev // NZH % NY, dev % NZH


def moved(value, to):
    n_isl, n_dev = lax.axis_size("island"), lax.axis_size("dev")
    pairs = []
    for i in range(n_isl * n_dev):
        target = to(*coords(i, n_dev))
        if target is not None:
            isl, x, y, zh = target
            pairs.append(
                (i, (isl % n_isl) * n_dev + ((x % NX) * NY + y % NY) * NZH + zh % NZH)
            )
    return lax.ppermute(value, AXES, pairs)


def place():
    isl = lax.axis_index("island").astype(jnp.int32)
    dev = lax.axis_index("dev").astype(jnp.int32)
    return dev >> 4, (dev >> 1) & 7, dev & 1, isl & 1, isl


def ordered(y, c, mine, other, out, at):
    for half in range(2):
        slabs = []
        for yy in range(half * 4, half * 4 + 4):
            j = (y - yy) & 7
            far = (j >= 4).astype(jnp.int32)
            pos = jnp.where(j < 4, j, 7 - j)
            slab = jnp.where(far == c, mine[pos], other[pos])
            slabs.append(slab.astype(jnp.float32))
        block = jnp.concatenate(slabs, axis=0).astype(jnp.bfloat16)
        out[pl.ds(at + half * 144, 144), :] = block


def column_kernel(mine, other, out):
    _, y, _, c, _ = place()
    ordered(y, c, mine, other, out, 0)


def column(mine, other):
    width = mine.shape[-1]
    return pl.pallas_call(
        column_kernel,
        out_shape=jax.ShapeDtypeStruct((NY * 36, width), jnp.bfloat16),
        cost_estimate=pl.CostEstimate(
            flops=NY * 36 * width, bytes_accessed=4 * NY * 36 * width, transcendentals=0
        ),
    )(mine, other)


def unit_kernel(im0, im1, wrap, im2, im3, out, raw, sems):
    rows = im0.shape[0]
    last = place()[4] == lax.axis_size("island") - 1
    copies = [
        pltpu.make_async_copy(src, raw.at[k], sems.at[k])
        for k, src in enumerate((im0, im1, im2, im3))
    ]
    for k in (0, 2, 3):
        copies[k].start()

    @pl.when(last)
    def _():
        pltpu.make_async_copy(wrap, raw.at[1], sems.at[1]).start()

    @pl.when(jnp.logical_not(last))
    def _():
        copies[1].start()

    for k in (0, 2, 3, 1):
        copies[k].wait()
        f = raw[k].astype(jnp.float32)
        s = lax.rsqrt(jnp.sum(f * f, axis=1, keepdims=True) + norm_eps)
        out[pl.ds(k * rows, rows), :] = (f * s).astype(jnp.bfloat16)


def tail_kernel(scal, unit, text, col, xcol, ocol, mcol, out_ref, full, hid, sems):
    x, _, _, c, _ = place()
    rows = out_ref.shape[0]
    step = jnp.where(c == 0, NX - 1, 1)
    wheres = (x, (x + step) & 3, (x + NX - step) & 3, (x + 2) & 3)
    copies = [
        pltpu.make_async_copy(src, full.at[pl.ds(pl.multiple_of(at * 288, 288), 288)], sems.at[k])
        for k, (src, at) in enumerate(zip((col, xcol, ocol, mcol), wheres))
    ]
    for copy in copies:
        copy.start()
    for copy in copies:
        copy.wait()
    hidden = jnp.dot(text[...], full[...], preferred_element_type=jnp.float32)
    inv = lax.rsqrt(jnp.sum(hidden * hidden, axis=1, keepdims=True) + norm_eps)
    hid[...] = hidden * inv
    text_b = hid[...].astype(jnp.bfloat16)
    scale, bias = scal[0], scal[1]
    scores = scale * lax.dot_general(
        text_b, unit[...], (((1,), (1,)), ((), ())), preferred_element_type=jnp.float32
    ) + bias
    r = lax.broadcasted_iota(jnp.int32, scores.shape, 0)
    s = lax.broadcasted_iota(jnp.int32, scores.shape, 1)
    probs = jax.nn.sigmoid(scores) - (r == s).astype(jnp.float32)
    grad = scale * jnp.dot(
        probs.astype(jnp.bfloat16), unit[...], preferred_element_type=jnp.float32
    )
    unit_txt = hid[...]
    radial = jnp.sum(unit_txt * grad, axis=1, keepdims=True)
    grad_hidden = ((grad - unit_txt * radial) * inv).astype(jnp.bfloat16)
    out_ref[...] = lax.dot_general(
        grad_hidden, full[...], (((1,), (1,)), ((), ())), preferred_element_type=jnp.float32
    ).astype(jnp.bfloat16)


def body(image_embed, text_feat, text_proj, log_scale, bias):
    rows, width = text_feat.shape
    x, y, zh, c, isl = place()
    n_isl = lax.axis_size("island")
    vmem = pl.BlockSpec(memory_space=pltpu.VMEM)
    smem = pl.BlockSpec(memory_space=pltpu.SMEM)
    anyw = pl.BlockSpec(memory_space=pl.ANY)

    far = moved(text_proj, lambda i, x, y, z: (i ^ 8, x, y - i % 2, 1 - z))
    near = moved(text_proj, lambda i, x, y, z: (i, x, y - 1, z) if i % 2 else None)
    base = jnp.where(c == 0, text_proj, near)
    pair = jnp.where(
        zh == 0, jnp.concatenate([base, far]), jnp.concatenate([far, base])
    )

    wrap2 = moved(image_embed, lambda i, x, y, z: (i - 2, x, y, z) if i < 2 else None)
    wrap3 = moved(image_embed, lambda i, x, y, z: (i - 3, x, y, z) if i == 2 else None)
    wrap2, wrap3 = lax.optimization_barrier((wrap2, wrap3))
    held = lax.optimization_barrier((image_embed, far))[0]
    near2 = moved(held, lambda i, x, y, z: (i - 2, x, y, z) if i >= 2 else None)
    two = jnp.where(isl >= n_isl - 2, wrap2, near2)

    got = [
        moved(pair, lambda i, x, y, z, k=k: (i, x, y + (-k if i % 2 else k), z))
        for k in (1, 2, 3)
    ]
    mine = jnp.stack([pair] + got)
    mid = moved(mine, lambda i, x, y, z: (i, x + 2, y, z))
    other = moved(mine, lambda i, x, y, z: (i ^ 1, x, y, z))
    col = column(mine, other)
    xcol = moved(col, lambda i, x, y, z: (i, x + (-1 if i % 2 else 1), y, z))
    two_ = lax.optimization_barrier((two, col))[0]
    one = moved(
        jnp.where(c == 0, two_, image_embed),
        lambda i, x, y, z: (i - 1, x, y, z) if i > 0 else None,
    )
    swapped = moved(two_, lambda i, x, y, z: (i ^ 1, x, y, z))
    mid_ = lax.optimization_barrier((mid, swapped))[0]
    omid = moved(mid_, lambda i, x, y, z: (i ^ 1, x, y, z))
    mcol = column(mid, omid)
    xcol_ = lax.optimization_barrier((xcol, mcol, one))[0]
    ocol = moved(xcol_, lambda i, x, y, z: (i ^ 1, x, y, z))

    unit = pl.pallas_call(
        unit_kernel,
        out_shape=jax.ShapeDtypeStruct((4 * rows, width), jnp.bfloat16),
        in_specs=[anyw] * 5,
        out_specs=vmem,
        scratch_shapes=[
            pltpu.VMEM((4, rows, width), jnp.bfloat16),
            pltpu.SemaphoreType.DMA((4,)),
        ],
        compiler_params=pltpu.CompilerParams(vmem_limit_bytes=16 * 1024 * 1024),
        cost_estimate=pl.CostEstimate(
            flops=12 * rows * width, bytes_accessed=16 * rows * width, transcendentals=4 * rows
        ),
    )(image_embed, one, wrap3, two, swapped)
    scal = jnp.stack([jnp.exp(log_scale), bias])
    return pl.pallas_call(
        tail_kernel,
        out_shape=jax.ShapeDtypeStruct((rows, width), jnp.bfloat16),
        in_specs=[smem, vmem, vmem] + [anyw] * 4,
        out_specs=vmem,
        scratch_shapes=[
            pltpu.VMEM((width, width), jnp.bfloat16),
            pltpu.VMEM((rows, width), jnp.float32),
            pltpu.SemaphoreType.DMA((4,)),
        ],
        compiler_params=pltpu.CompilerParams(vmem_limit_bytes=24 * 1024 * 1024),
        cost_estimate=pl.CostEstimate(
            flops=2 * 2 * rows * width * (width + 4 * rows),
            bytes_accessed=8 * 1024 * 1024,
            transcendentals=4 * rows * rows,
        ),
    )(scal, unit, text_feat, col, xcol, ocol, mcol)


def solution(mesh):
    placed = (P(AXES, None), P(AXES, None), P("dev", None), P(), P())
    return jax.shard_map(
        body, mesh=mesh, in_specs=placed, out_specs=P(AXES, None), check_vma=False
    )
```

time: 94.7 us -> 90.3 us (0.954)
  the two profiles are of different devices: /device:TPU:9 before, /device:TPU:1 now
where the time goes in v2:
time: 90.3 us; the launch traced here: 89.7 us
  starting transfers between devices  65.2 us (72%)
  Pallas kernels  12.3 us (14%)
  waiting for transfers between devices  7.74 us (9%)
  between operations  1.63 us (2%)
  local copies, waits for them, and re-layouts  1.59 us (2%)
  other arithmetic  1.22 us (1%)
    ppermute x15, starting transfers between devices, moved(): return lax.ppermute(value, AXES, pairs)  65.2 us
    ppermute x15, waiting for transfers between devices, moved(): return lax.ppermute(value, AXES, pairs)  7.74 us
    pallas_call x1, Pallas kernels, body(): pl.pallas_call(tail_kernel, out_shape=jax.ShapeDtypeStruct((rows, width),...  6.74 us
    pallas_call x2, Pallas kernels, column(): pl.pallas_call(column_kernel, out_shape=jax.ShapeDtypeStruct((NY * 36, wi...  4.23 us
  transfers between devices with their start and end apart: 15, of which 5 were waited for; matrix products, arithmetic and copies ran while one was open for 1% of the time, Pallas kernels for 6%

profile of v2, /device:TPU:1, one launch (start us, length us, event | category | flops | bytes accessed | tf_op | source)
XLA Modules:
  0.0 89.7 jit_solution(2287576114936421694)
XLA Ops:
  0.0 0.0 copy-start
  0.0 6.0 %collective-permute-start.4 = (bf16[18,1152]{1,0:T(8,128)(2,1)}, bf16[18,1152]{1,0:T(8,128)(2,1)S(1)}, u32[]{:S(2)}, u32[]{:S(2)}) collective-permute-start(bf16[18,1152]{1,0:T(8,128)(2,1)} %param.7), channel_id=1, source_target_pairs={{64,78},{65,79},{66,64},{67,65},{68,66},{69,67},{70,68},{71,69},{7... | collective-permute-start | bytes 124424 | tf_op jit(solution)/shard_map/ppermute | solution.py:28
  6.1 18.7 %collective-permute-start.2 = (bf16[18,1152]{1,0:T(8,128)(2,1)}, bf16[18,1152]{1,0:T(8,128)(2,1)S(1)}, u32[]{:S(2)}, u32[]{:S(2)}) collective-permute-start(bf16[18,1152]{1,0:T(8,128)(2,1)} %param.7), channel_id=1, source_target_pairs={{0,513},{1,512},{2,515},{3,514},{4,517},{5,516},{6,519},{7,518},{8... | collective-permute-start | bytes 124424 | tf_op jit(solution)/shard_map/ppermute | solution.py:28
  24.8 0.0 collective-permute-done.4
  24.8 1.5 %collective-permute-done.2 = bf16[18,1152]{1,0:T(8,128)(2,1)S(1)} collective-permute-done((bf16[18,1152]{1,0:T(8,128)(2,1)}, bf16[18,1152]{1,0:T(8,128)(2,1)S(1)}, u32[]{:S(2)}, u32[]{:S(2)}) %collective-permute-start.2) | collective-permute-done | bytes 41504 | tf_op jit(solution)/shard_map/ppermute | solution.py:28
  26.3 6.9 %collective-permute-start.7 = (bf16[36,1152]{1,0:T(8,128)(2,1)S(1)}, bf16[36,1152]{1,0:T(8,128)(2,1)S(1)}, u32[]{:S(2)}, u32[]{:S(2)}) collective-permute-start(bf16[36,1152]{1,0:T(8,128)(2,1)S(1)} %maximum_select_fusion.1), channel_id=1, source_target_pairs={{0,6},{1,7},{2,8},{3,9},{4,10},{5,11},{6,12},{7,13},{8,14},{9,15},... | collective-permute-start | bytes 248840 | tf_op jit(solution)/shard_map/ppermute | solution.py:28
  33.3 5.8 %collective-permute-start = (bf16[256,1152]{1,0:T(8,128)(2,1)}, bf16[256,1152]{1,0:T(8,128)(2,1)S(1)}, u32[]{:S(2)}, u32[]{:S(2)}) collective-permute-start(bf16[256,1152]{1,0:T(8,128)(2,1)} %im0.1), channel_id=1, source_target_pairs={{0,896},{1,897},{2,898},{3,899},{4,900},{5,901},{6,902},{7,903},{8... | collective-permute-start | bytes 1769480 | tf_op jit(solution)/shard_map/ppermute | solution.py:28
  39.1 0.7 collective-permute-start.1
  39.8 2.9 %collective-permute-start.6 = (bf16[36,1152]{1,0:T(8,128)(2,1)S(1)}, bf16[36,1152]{1,0:T(8,128)(2,1)S(1)}, u32[]{:S(2)}, u32[]{:S(2)}) collective-permute-start(bf16[36,1152]{1,0:T(8,128)(2,1)S(1)} %maximum_select_fusion.1), channel_id=1, source_target_pairs={{0,4},{1,5},{2,6},{3,7},{4,8},{5,9},{6,10},{7,11},{8,12},{9,13},{1... | collective-permute-start | bytes 248840 | tf_op jit(solution)/shard_map/ppermute | solution.py:28
  42.7 2.1 %collective-permute-start.5 = (bf16[36,1152]{1,0:T(8,128)(2,1)S(1)}, bf16[36,1152]{1,0:T(8,128)(2,1)S(1)}, u32[]{:S(2)}, u32[]{:S(2)}) collective-permute-start(bf16[36,1152]{1,0:T(8,128)(2,1)S(1)} %maximum_select_fusion.1), channel_id=1, source_target_pairs={{0,2},{1,3},{2,4},{3,5},{4,6},{5,7},{6,8},{7,9},{8,10},{9,11},{10,... | collective-permute-start | bytes 248840 | tf_op jit(solution)/shard_map/ppermute | solution.py:28
  44.7 0.0 collective-permute-done.7
  44.7 1.3 %collective-permute-start.3 = (bf16[256,1152]{1,0:T(8,128)(2,1)}, bf16[256,1152]{1,0:T(8,128)(2,1)S(1)}, u32[]{:S(2)}, u32[]{:S(2)}) collective-permute-start(bf16[256,1152]{1,0:T(8,128)(2,1)} %im0.1), channel_id=1, source_target_pairs={{128,0},{129,1},{130,2},{131,3},{132,4},{133,5},{134,6},{135,7},{1... | collective-permute-start | bytes 1769480 | tf_op jit(solution)/shard_map/ppermute | solution.py:28
  46.1 1.2 %collective-permute-done.6 = bf16[36,1152]{1,0:T(8,128)(2,1)S(1)} collective-permute-done((bf16[36,1152]{1,0:T(8,128)(2,1)S(1)}, bf16[36,1152]{1,0:T(8,128)(2,1)S(1)}, u32[]{:S(2)}, u32[]{:S(2)}) %collective-permute-start.6) | collective-permute-done | bytes 82976 | tf_op jit(solution)/shard_map/ppermute | solution.py:28
  47.3 0.9 collective-permute-done.5
  48.1 0.1 pad_maximum_fusion.mine
  48.2 0.0 copy-start.4
  48.2 5.3 %collective-permute-start.8 = (bf16[4,36,1152]{2,1,0:T(8,128)(2,1)S(1)}, bf16[4,36,1152]{2,1,0:T(8,128)(2,1)S(1)}, u32[]{:S(2)}, u32[]{:S(2)}) collective-permute-start(bf16[4,36,1152]{2,1,0:T(8,128)(2,1)S(1)} %pad_maximum_fusion.mine), channel_id=1, source_target_pairs={{0,64},{1,65},{2,66},{3,67},{4,68},{5,69},{6,70},{7,71},{8,72},{9,... | collective-permute-start | bytes 995336 | tf_op jit(solution)/shard_map/ppermute | solution.py:28
  53.5 4.7 %collective-permute-start.12 = (bf16[4,36,1152]{2,1,0:T(8,128)(2,1)S(1)}, bf16[4,36,1152]{2,1,0:T(8,128)(2,1)}, u32[]{:S(2)}, u32[]{:S(2)}) collective-permute-start(bf16[4,36,1152]{2,1,0:T(8,128)(2,1)S(1)} %pad_maximum_fusion.mine), channel_id=1, source_target_pairs={{0,32},{1,33},{2,34},{3,35},{4,36},{5,37},{6,38},{7,39},{8,40},{9,... | collective-permute-start | bytes 995336 | tf_op jit(solution)/shard_map/ppermute | solution.py:28
  58.2 0.0 collective-permute-done.8.other
  58.2 0.0 copy-done.4
  58.2 0.0 copy-start.5
  58.2 0.7 copy-done.5
  58.9 2.1 %shard_map.55.col = bf16[288,1152]{1,0:T(8,128)(2,1)} custom-call(bf16[4,36,1152]{2,1,0:T(8,128)(2,1)} %copy-done.4, bf16[4,36,1152]{2,1,0:T(8,128)(2,1)} %copy-done.5), custom_call_target="tpu_custom_call" | custom-call | flops 331776 | bytes 1327104 | tf_op jit(solution)/shard_map/pallas_call | solution.py:57
  61.0 2.8 %collective-permute-start.11 = (bf16[288,1152]{1,0:T(8,128)(2,1)}, bf16[288,1152]{1,0:T(8,128)(2,1)}, u32[]{:S(2)}, u32[]{:S(2)}) collective-permute-start(bf16[288,1152]{1,0:T(8,128)(2,1)} %shard_map.55.col), channel_id=1, source_target_pairs={{0,16},{1,17},{2,18},{3,19},{4,20},{5,21},{6,22},{7,23},{8,24},{9,... | collective-permute-start | bytes 1990664 | tf_op jit(solution)/shard_map/ppermute | solution.py:28
  63.8 0.0 collective-permute-done
  63.8 0.0 collective-permute-done.1.wrap
  63.8 0.0 collective-permute-done.3
  63.8 0.1 broadcast_select_fusion.im2
  63.9 1.9 %collective-permute-start.10 = (bf16[256,1152]{1,0:T(8,128)(2,1)S(1)}, bf16[256,1152]{1,0:T(8,128)(2,1)S(1)}, u32[]{:S(2)}, u32[]{:S(2)}) collective-permute-start(bf16[256,1152]{1,0:T(8,128)(2,1)S(1)} %broadcast_select_fusion.im2), channel_id=1, source_target_pairs={{0,64},{1,65},{2,66},{3,67},{4,68},{5,69},{6,70},{7,71},{8,72},{9,... | collective-permute-start | bytes 1769480 | tf_op jit(solution)/shard_map/ppermute | solution.py:28
  65.9 0.0 copy-done
  65.9 0.9 broadcast_select_fusion.1
  66.7 2.4 %collective-permute-start.9 = (bf16[256,1152]{1,0:T(8,128)(2,1)}, bf16[256,1152]{1,0:T(8,128)(2,1)S(1)}, u32[]{:S(2)}, u32[]{:S(2)}) collective-permute-start(bf16[256,1152]{1,0:T(8,128)(2,1)} %broadcast_select_fusion.1), channel_id=1, source_target_pairs={{64,0},{65,1},{66,2},{67,3},{68,4},{69,5},{70,6},{71,7},{72,8},{73... | collective-permute-start | bytes 1769480 | tf_op jit(solution)/shard_map/ppermute | solution.py:28
  69.1 0.0 collective-permute-done.12.mine
  69.1 0.0 collective-permute-done.10.im3
  69.2 1.9 %collective-permute-start.13 = (bf16[4,36,1152]{2,1,0:T(8,128)(2,1)}, bf16[4,36,1152]{2,1,0:T(8,128)(2,1)S(1)}, u32[]{:S(2)}, u32[]{:S(2)}) collective-permute-start(bf16[4,36,1152]{2,1,0:T(8,128)(2,1)} %collective-permute-done.12.mine), channel_id=1, source_target_pairs={{0,64},{1,65},{2,66},{3,67},{4,68},{5,69},{6,70},{7,71},{8,72},{9,... | collective-permute-start | bytes 995336 | tf_op jit(solution)/shard_map/ppermute | solution.py:28
  71.1 1.9 %collective-permute-done.13.other = bf16[4,36,1152]{2,1,0:T(8,128)(2,1)S(1)} collective-permute-done((bf16[4,36,1152]{2,1,0:T(8,128)(2,1)}, bf16[4,36,1152]{2,1,0:T(8,128)(2,1)S(1)}, u32[]{:S(2)}, u32[]{:S(2)}) %collective-permute-start.13) | collective-permute-done | bytes 331808 | tf_op jit(solution)/shard_map/ppermute | solution.py:28
  73.0 0.7 copy-done.6
  73.7 2.1 %shard_map.57.mcol = bf16[288,1152]{1,0:T(8,128)(2,1)} custom-call(bf16[4,36,1152]{2,1,0:T(8,128)(2,1)} %collective-permute-done.12.mine, bf16[4,36,1152]{2,1,0:T(8,128)(2,1)} %copy-done.6), custom_call_target="tpu_custom_call" | custom-call | flops 331776 | bytes 1327104 | tf_op jit(solution)/shard_map/pallas_call | solution.py:57
  75.8 0.0 collective-permute-done.11.xcol
  75.8 2.3 %collective-permute-done.9.im1 = bf16[256,1152]{1,0:T(8,128)(2,1)S(1)} collective-permute-done((bf16[256,1152]{1,0:T(8,128)(2,1)}, bf16[256,1152]{1,0:T(8,128)(2,1)S(1)}, u32[]{:S(2)}, u32[]{:S(2)}) %collective-permute-start.9) | collective-permute-done | bytes 589856 | tf_op jit(solution)/shard_map/ppermute | solution.py:28
  78.2 1.9 %collective-permute-start.14 = (bf16[288,1152]{1,0:T(8,128)(2,1)}, bf16[288,1152]{1,0:T(8,128)(2,1)}, u32[]{:S(2)}, u32[]{:S(2)}) collective-permute-start(bf16[288,1152]{1,0:T(8,128)(2,1)} %collective-permute-done.11.xcol), channel_id=1, source_target_pairs={{0,64},{1,65},{2,66},{3,67},{4,68},{5,69},{6,70},{7,71},{8,72},{9,... | collective-permute-start | bytes 1990664 | tf_op jit(solution)/shard_map/ppermute | solution.py:28
  81.4 0.1 pad_maximum_fusion.1.scal
  81.5 1.3 %shard_map.56.unit = bf16[1024,1152]{1,0:T(8,128)(2,1)S(1)} custom-call(bf16[256,1152]{1,0:T(8,128)(2,1)S(1)} %copy-done, bf16[256,1152]{1,0:T(8,128)(2,1)S(1)} %collective-permute-done.9.im1, bf16[256,1152]{1,0:T(8,128)(2,1)S(1)} %collective-permute-done.1.wrap, bf16[256,1152]{1,0:T(8,128)(2,1)S(1)} %broadcast_select_fusion.im2, ...), custom_call_target="tpu_custom_call" | custom-call | flops 3538944 | bytes 4718592 | tf_op jit(solution)/shard_map/pallas_call | solution.py:169
  82.8 0.0 collective-permute-done.14.ocol
  82.8 0.0 copy-done.1
  82.8 0.0 copy-done.2
  82.9 0.1 copy-done.3
  82.9 6.7 %shard_map.58 = bf16[256,1152]{1,0:T(8,128)(2,1)} custom-call(f32[2]{0:T(128)S(1)} %pad_maximum_fusion.1.scal, bf16[1024,1152]{1,0:T(8,128)(2,1)S(1)} %shard_map.56.unit, bf16[256,1152]{1,0:T(8,128)(2,1)S(1)} %copy-done.3, bf16[288,1152]{1,0:T(8,128)(2,1)S(1)} %copy-done.1, bf16[288,1152]{1,0:T(8,128)(2,1)} %collective-permute-done.11.xcol, ...), custom_call_target="tpu_custom_call" | custom-call | flops 2566914048 | bytes 8388608 | tf_op jit(solution)/shard_map/pallas_call | solution.py:184
  (7 shorter events, 0.1 us)
Async XLA Ops:
  0.0 65.9 %copy-start = (bf16[256,1152]{1,0:T(8,128)(2,1)S(1)}, bf16[256,1152]{1,0:T(8,128)(2,1)}, u32[]{:S(2)}) copy-start(bf16[256,1152]{1,0:T(8,128)(2,1)} %im0.1) | copy-start | bytes 1769476
  0.0 24.8 %collective-permute-start.4 = (bf16[18,1152]{1,0:T(8,128)(2,1)}, bf16[18,1152]{1,0:T(8,128)(2,1)S(1)}, u32[]{:S(2)}, u32[]{:S(2)}) collective-permute-start(bf16[18,1152]{1,0:T(8,128)(2,1)} %param.7), channel_id=1, source_target_pairs={{64,78},{65,79},{66,64},{67,65},{68,66},{69,67},{70,68},{71,69},{7... | collective-permute-start | bytes 124424 | tf_op jit(solution)/shard_map/ppermute | solution.py:28
  6.1 20.2 %collective-permute-start.2 = (bf16[18,1152]{1,0:T(8,128)(2,1)}, bf16[18,1152]{1,0:T(8,128)(2,1)S(1)}, u32[]{:S(2)}, u32[]{:S(2)}) collective-permute-start(bf16[18,1152]{1,0:T(8,128)(2,1)} %param.7), channel_id=1, source_target_pairs={{0,513},{1,512},{2,515},{3,514},{4,517},{5,516},{6,519},{7,518},{8... | collective-permute-start | bytes 124424 | tf_op jit(solution)/shard_map/ppermute | solution.py:28
  26.3 18.4 %collective-permute-start.7 = (bf16[36,1152]{1,0:T(8,128)(2,1)S(1)}, bf16[36,1152]{1,0:T(8,128)(2,1)S(1)}, u32[]{:S(2)}, u32[]{:S(2)}) collective-permute-start(bf16[36,1152]{1,0:T(8,128)(2,1)S(1)} %maximum_select_fusion.1), channel_id=1, source_target_pairs={{0,6},{1,7},{2,8},{3,9},{4,10},{5,11},{6,12},{7,13},{8,14},{9,15},... | collective-permute-start | bytes 248840 | tf_op jit(solution)/shard_map/ppermute | solution.py:28
  33.3 30.5 %collective-permute-start = (bf16[256,1152]{1,0:T(8,128)(2,1)}, bf16[256,1152]{1,0:T(8,128)(2,1)S(1)}, u32[]{:S(2)}, u32[]{:S(2)}) collective-permute-start(bf16[256,1152]{1,0:T(8,128)(2,1)} %im0.1), channel_id=1, source_target_pairs={{0,896},{1,897},{2,898},{3,899},{4,900},{5,901},{6,902},{7,903},{8... | collective-permute-start | bytes 1769480 | tf_op jit(solution)/shard_map/ppermute | solution.py:28
  39.1 24.7 %collective-permute-start.1 = (bf16[256,1152]{1,0:T(8,128)(2,1)}, bf16[256,1152]{1,0:T(8,128)(2,1)S(1)}, u32[]{:S(2)}, u32[]{:S(2)}) collective-permute-start(bf16[256,1152]{1,0:T(8,128)(2,1)} %im0.1), channel_id=1, source_target_pairs={{128,960},{129,961},{130,962},{131,963},{132,964},{133,965},{134,9... | collective-permute-start | bytes 1769480 | tf_op jit(solution)/shard_map/ppermute | solution.py:28
  39.8 7.5 %collective-permute-start.6 = (bf16[36,1152]{1,0:T(8,128)(2,1)S(1)}, bf16[36,1152]{1,0:T(8,128)(2,1)S(1)}, u32[]{:S(2)}, u32[]{:S(2)}) collective-permute-start(bf16[36,1152]{1,0:T(8,128)(2,1)S(1)} %maximum_select_fusion.1), channel_id=1, source_target_pairs={{0,4},{1,5},{2,6},{3,7},{4,8},{5,9},{6,10},{7,11},{8,12},{9,13},{1... | collective-permute-start | bytes 248840 | tf_op jit(solution)/shard_map/ppermute | solution.py:28
  42.7 5.5 %collective-permute-start.5 = (bf16[36,1152]{1,0:T(8,128)(2,1)S(1)}, bf16[36,1152]{1,0:T(8,128)(2,1)S(1)}, u32[]{:S(2)}, u32[]{:S(2)}) collective-permute-start(bf16[36,1152]{1,0:T(8,128)(2,1)S(1)} %maximum_select_fusion.1), channel_id=1, source_target_pairs={{0,2},{1,3},{2,4},{3,5},{4,6},{5,7},{6,8},{7,9},{8,10},{9,11},{10,... | collective-permute-start | bytes 248840 | tf_op jit(solution)/shard_map/ppermute | solution.py:28
  44.7 19.1 %collective-permute-start.3 = (bf16[256,1152]{1,0:T(8,128)(2,1)}, bf16[256,1152]{1,0:T(8,128)(2,1)S(1)}, u32[]{:S(2)}, u32[]{:S(2)}) collective-permute-start(bf16[256,1152]{1,0:T(8,128)(2,1)} %im0.1), channel_id=1, source_target_pairs={{128,0},{129,1},{130,2},{131,3},{132,4},{133,5},{134,6},{135,7},{1... | collective-permute-start | bytes 1769480 | tf_op jit(solution)/shard_map/ppermute | solution.py:28
  48.2 10.0 %copy-start.4 = (bf16[4,36,1152]{2,1,0:T(8,128)(2,1)}, bf16[4,36,1152]{2,1,0:T(8,128)(2,1)S(1)}, u32[]{:S(2)}) copy-start(bf16[4,36,1152]{2,1,0:T(8,128)(2,1)S(1)} %pad_maximum_fusion.mine) | copy-start | bytes 995332
  48.2 9.9 %collective-permute-start.8 = (bf16[4,36,1152]{2,1,0:T(8,128)(2,1)S(1)}, bf16[4,36,1152]{2,1,0:T(8,128)(2,1)S(1)}, u32[]{:S(2)}, u32[]{:S(2)}) collective-permute-start(bf16[4,36,1152]{2,1,0:T(8,128)(2,1)S(1)} %pad_maximum_fusion.mine), channel_id=1, source_target_pairs={{0,64},{1,65},{2,66},{3,67},{4,68},{5,69},{6,70},{7,71},{8,72},{9,... | collective-permute-start | bytes 995336 | tf_op jit(solution)/shard_map/ppermute | solution.py:28
  53.5 15.6 %collective-permute-start.12 = (bf16[4,36,1152]{2,1,0:T(8,128)(2,1)S(1)}, bf16[4,36,1152]{2,1,0:T(8,128)(2,1)}, u32[]{:S(2)}, u32[]{:S(2)}) collective-permute-start(bf16[4,36,1152]{2,1,0:T(8,128)(2,1)S(1)} %pad_maximum_fusion.mine), channel_id=1, source_target_pairs={{0,32},{1,33},{2,34},{3,35},{4,36},{5,37},{6,38},{7,39},{8,40},{9,... | collective-permute-start | bytes 995336 | tf_op jit(solution)/shard_map/ppermute | solution.py:28
  58.2 0.7 copy-start.5
  61.0 14.8 %collective-permute-start.11 = (bf16[288,1152]{1,0:T(8,128)(2,1)}, bf16[288,1152]{1,0:T(8,128)(2,1)}, u32[]{:S(2)}, u32[]{:S(2)}) collective-permute-start(bf16[288,1152]{1,0:T(8,128)(2,1)} %shard_map.55.col), channel_id=1, source_target_pairs={{0,16},{1,17},{2,18},{3,19},{4,20},{5,21},{6,22},{7,23},{8,24},{9,... | collective-permute-start | bytes 1990664 | tf_op jit(solution)/shard_map/ppermute | solution.py:28
  63.9 5.2 %collective-permute-start.10 = (bf16[256,1152]{1,0:T(8,128)(2,1)S(1)}, bf16[256,1152]{1,0:T(8,128)(2,1)S(1)}, u32[]{:S(2)}, u32[]{:S(2)}) collective-permute-start(bf16[256,1152]{1,0:T(8,128)(2,1)S(1)} %broadcast_select_fusion.im2), channel_id=1, source_target_pairs={{0,64},{1,65},{2,66},{3,67},{4,68},{5,69},{6,70},{7,71},{8,72},{9,... | collective-permute-start | bytes 1769480 | tf_op jit(solution)/shard_map/ppermute | solution.py:28
  66.7 11.4 %collective-permute-start.9 = (bf16[256,1152]{1,0:T(8,128)(2,1)}, bf16[256,1152]{1,0:T(8,128)(2,1)S(1)}, u32[]{:S(2)}, u32[]{:S(2)}) collective-permute-start(bf16[256,1152]{1,0:T(8,128)(2,1)} %broadcast_select_fusion.1), channel_id=1, source_target_pairs={{64,0},{65,1},{66,2},{67,3},{68,4},{69,5},{70,6},{71,7},{72,8},{73... | collective-permute-start | bytes 1769480 | tf_op jit(solution)/shard_map/ppermute | solution.py:28
  69.2 3.8 %collective-permute-start.13 = (bf16[4,36,1152]{2,1,0:T(8,128)(2,1)}, bf16[4,36,1152]{2,1,0:T(8,128)(2,1)S(1)}, u32[]{:S(2)}, u32[]{:S(2)}) collective-permute-start(bf16[4,36,1152]{2,1,0:T(8,128)(2,1)} %collective-permute-done.12.mine), channel_id=1, source_target_pairs={{0,64},{1,65},{2,66},{3,67},{4,68},{5,69},{6,70},{7,71},{8,72},{9,... | collective-permute-start | bytes 995336 | tf_op jit(solution)/shard_map/ppermute | solution.py:28
  73.0 0.7 copy-start.6
  78.2 4.7 %collective-permute-start.14 = (bf16[288,1152]{1,0:T(8,128)(2,1)}, bf16[288,1152]{1,0:T(8,128)(2,1)}, u32[]{:S(2)}, u32[]{:S(2)}) collective-permute-start(bf16[288,1152]{1,0:T(8,128)(2,1)} %collective-permute-done.11.xcol), channel_id=1, source_target_pairs={{0,64},{1,65},{2,66},{3,67},{4,68},{5,69},{6,70},{7,71},{8,72},{9,... | collective-permute-start | bytes 1990664 | tf_op jit(solution)/shard_map/ppermute | solution.py:28
  81.5 1.4 %copy-start.1 = (bf16[288,1152]{1,0:T(8,128)(2,1)S(1)}, bf16[288,1152]{1,0:T(8,128)(2,1)}, u32[]{:S(2)}) copy-start(bf16[288,1152]{1,0:T(8,128)(2,1)} %shard_map.55.col) | copy-start | bytes 1990660
  81.5 1.4 %copy-start.2 = (bf16[288,1152]{1,0:T(8,128)(2,1)S(1)}, bf16[288,1152]{1,0:T(8,128)(2,1)}, u32[]{:S(2)}) copy-start(bf16[288,1152]{1,0:T(8,128)(2,1)} %shard_map.57.mcol) | copy-start | bytes 1990660
  81.5 1.5 %copy-start.3 = (bf16[256,1152]{1,0:T(8,128)(2,1)S(1)}, bf16[256,1152]{1,0:T(8,128)(2,1)}, u32[]{:S(2)}) copy-start(bf16[256,1152]{1,0:T(8,128)(2,1)} %text.1) | copy-start | bytes 1769476

commit v3 on v2

--- a/solution.py
+++ b/solution.py
@@ -141,8 +141,8 @@
     wrap2 = moved(image_embed, lambda i, x, y, z: (i - 2, x, y, z) if i < 2 else None)
     wrap3 = moved(image_embed, lambda i, x, y, z: (i - 3, x, y, z) if i == 2 else None)
     wrap2, wrap3 = lax.optimization_barrier((wrap2, wrap3))
-    held = lax.optimization_barrier((image_embed, far))[0]
-    near2 = moved(held, lambda i, x, y, z: (i - 2, x, y, z) if i >= 2 else None)
+    img = lax.optimization_barrier((image_embed, far))[0]
+    near2 = moved(img, lambda i, x, y, z: (i - 2, x, y, z) if i >= 2 else None)
     two = jnp.where(isl >= n_isl - 2, wrap2, near2)
 
     got = [
@@ -150,6 +150,7 @@
         for k in (1, 2, 3)
     ]
     mine = jnp.stack([pair] + got)
+    mine = lax.optimization_barrier((mine, wrap2))[0]
     mid = moved(mine, lambda i, x, y, z: (i, x + 2, y, z))
     other = moved(mine, lambda i, x, y, z: (i ^ 1, x, y, z))
     col = column(mine, other)
@@ -160,10 +161,10 @@
         lambda i, x, y, z: (i - 1, x, y, z) if i > 0 else None,
     )
     swapped = moved(two_, lambda i, x, y, z: (i ^ 1, x, y, z))
-    mid_ = lax.optimization_barrier((mid, swapped))[0]
+    mid_ = mid
     omid = moved(mid_, lambda i, x, y, z: (i ^ 1, x, y, z))
     mcol = column(mid, omid)
-    xcol_ = lax.optimization_barrier((xcol, mcol, one))[0]
+    xcol_ = lax.optimization_barrier((xcol, mcol, one, swapped))[0]
     ocol = moved(xcol_, lambda i, x, y, z: (i ^ 1, x, y, z))
 
     unit = pl.pallas_call(

time: 90.3 us -> 87.7 us (0.971)
  starting transfers between devices: 65.2 us -> 62.3 us
  waiting for transfers between devices: 7.74 us -> 8.86 us
    ppermute x15, starting transfers between devices: 65.2 us -> 62.3 us  [moved(): return lax.ppermute(value, AXES, pairs)]
    ppermute x15, waiting for transfers between devices: 7.74 us -> 8.86 us  [moved(): return lax.ppermute(value, AXES, pairs)]
  transfers between devices with their start and end apart: 15 -> 15, of which waited for: 5 -> 4; matrix products, arithmetic and copies ran while one was open for 1% -> 1% of each run, Pallas kernels for 6% -> 6%
where the time goes in v3:
time: 87.7 us; the launch traced here: 87.1 us
  starting transfers between devices  62.3 us (71%)
  Pallas kernels  12.2 us (14%)
  waiting for transfers between devices  8.86 us (10%)
  between operations  1.63 us (2%)
  other arithmetic  1.22 us (1%)
    ppermute x15, starting transfers between devices, moved(): return lax.ppermute(value, AXES, pairs)  62.3 us
    ppermute x15, waiting for transfers between devices, moved(): return lax.ppermute(value, AXES, pairs)  8.86 us
    pallas_call x1, Pallas kernels, body(): pl.pallas_call(tail_kernel, out_shape=jax.ShapeDtypeStruct((rows, width),...  6.72 us
    pallas_call x2, Pallas kernels, column(): pl.pallas_call(column_kernel, out_shape=jax.ShapeDtypeStruct((NY * 36, wi...  4.18 us
  transfers between devices with their start and end apart: 15, of which 4 were waited for; matrix products, arithmetic and copies ran while one was open for 1% of the time, Pallas kernels for 6%

profile of v3, /device:TPU:1, one launch (start us, length us, event | category | flops | bytes accessed | tf_op | source)
XLA Modules:
  0.0 87.1 jit_solution(8714290235982525327)
XLA Ops:
  0.0 0.0 copy-start
  0.0 21.8 %collective-permute-start.2 = (bf16[18,1152]{1,0:T(8,128)(2,1)}, bf16[18,1152]{1,0:T(8,128)(2,1)S(1)}, u32[]{:S(2)}, u32[]{:S(2)}) collective-permute-start(bf16[18,1152]{1,0:T(8,128)(2,1)} %param.7), channel_id=1, source_target_pairs={{0,513},{1,512},{2,515},{3,514},{4,517},{5,516},{6,519},{7,518},{8... | collective-permute-start | bytes 124424 | tf_op jit(solution)/shard_map/ppermute | solution.py:28
  21.8 3.0 %collective-permute-start.4 = (bf16[18,1152]{1,0:T(8,128)(2,1)}, bf16[18,1152]{1,0:T(8,128)(2,1)S(1)}, u32[]{:S(2)}, u32[]{:S(2)}) collective-permute-start(bf16[18,1152]{1,0:T(8,128)(2,1)} %param.7), channel_id=1, source_target_pairs={{64,78},{65,79},{66,64},{67,65},{68,66},{69,67},{70,68},{71,69},{7... | collective-permute-start | bytes 124424 | tf_op jit(solution)/shard_map/ppermute | solution.py:28
  24.8 6.1 %collective-permute-start = (bf16[256,1152]{1,0:T(8,128)(2,1)}, bf16[256,1152]{1,0:T(8,128)(2,1)S(1)}, u32[]{:S(2)}, u32[]{:S(2)}) collective-permute-start(bf16[256,1152]{1,0:T(8,128)(2,1)} %im0.1), channel_id=1, source_target_pairs={{0,896},{1,897},{2,898},{3,899},{4,900},{5,901},{6,902},{7,903},{8... | collective-permute-start | bytes 1769480 | tf_op jit(solution)/shard_map/ppermute | solution.py:28
  30.9 0.7 collective-permute-start.1
  31.6 0.0 collective-permute-done.2
  31.6 1.3 %collective-permute-start.3 = (bf16[256,1152]{1,0:T(8,128)(2,1)}, bf16[256,1152]{1,0:T(8,128)(2,1)S(1)}, u32[]{:S(2)}, u32[]{:S(2)}) collective-permute-start(bf16[256,1152]{1,0:T(8,128)(2,1)} %im0.1), channel_id=1, source_target_pairs={{128,0},{129,1},{130,2},{131,3},{132,4},{133,5},{134,6},{135,7},{1... | collective-permute-start | bytes 1769480 | tf_op jit(solution)/shard_map/ppermute | solution.py:28
  32.9 0.0 collective-permute-done.4
  33.0 3.6 %collective-permute-start.7 = (bf16[36,1152]{1,0:T(8,128)(2,1)S(1)}, bf16[36,1152]{1,0:T(8,128)(2,1)S(1)}, u32[]{:S(2)}, u32[]{:S(2)}) collective-permute-start(bf16[36,1152]{1,0:T(8,128)(2,1)S(1)} %maximum_select_fusion.1), channel_id=1, source_target_pairs={{0,6},{1,7},{2,8},{3,9},{4,10},{5,11},{6,12},{7,13},{8,14},{9,15},... | collective-permute-start | bytes 248840 | tf_op jit(solution)/shard_map/ppermute | solution.py:28
  36.7 2.0 %collective-permute-start.6 = (bf16[36,1152]{1,0:T(8,128)(2,1)S(1)}, bf16[36,1152]{1,0:T(8,128)(2,1)S(1)}, u32[]{:S(2)}, u32[]{:S(2)}) collective-permute-start(bf16[36,1152]{1,0:T(8,128)(2,1)S(1)} %maximum_select_fusion.1), channel_id=1, source_target_pairs={{0,4},{1,5},{2,6},{3,7},{4,8},{5,9},{6,10},{7,11},{8,12},{9,13},{1... | collective-permute-start | bytes 248840 | tf_op jit(solution)/shard_map/ppermute | solution.py:28
  38.7 2.0 %collective-permute-done.7 = bf16[36,1152]{1,0:T(8,128)(2,1)S(1)} collective-permute-done((bf16[36,1152]{1,0:T(8,128)(2,1)S(1)}, bf16[36,1152]{1,0:T(8,128)(2,1)S(1)}, u32[]{:S(2)}, u32[]{:S(2)}) %collective-permute-start.7) | collective-permute-done | bytes 82976 | tf_op jit(solution)/shard_map/ppermute | solution.py:28
  40.7 5.8 %collective-permute-start.5 = (bf16[36,1152]{1,0:T(8,128)(2,1)S(1)}, bf16[36,1152]{1,0:T(8,128)(2,1)S(1)}, u32[]{:S(2)}, u32[]{:S(2)}) collective-permute-start(bf16[36,1152]{1,0:T(8,128)(2,1)S(1)} %maximum_select_fusion.1), channel_id=1, source_target_pairs={{0,2},{1,3},{2,4},{3,5},{4,6},{5,7},{6,8},{7,9},{8,10},{9,11},{10,... | collective-permute-start | bytes 248840 | tf_op jit(solution)/shard_map/ppermute | solution.py:28
  46.6 0.0 collective-permute-done.6
  46.6 1.5 %collective-permute-done.5 = bf16[36,1152]{1,0:T(8,128)(2,1)S(1)} collective-permute-done((bf16[36,1152]{1,0:T(8,128)(2,1)S(1)}, bf16[36,1152]{1,0:T(8,128)(2,1)S(1)}, u32[]{:S(2)}, u32[]{:S(2)}) %collective-permute-start.5) | collective-permute-done | bytes 82976 | tf_op jit(solution)/shard_map/ppermute | solution.py:28
  48.1 0.1 pad_maximum_fusion.mine
  48.1 0.0 copy-start.4
  48.2 0.0 collective-permute-done
  48.2 0.0 collective-permute-done.1.wrap
  48.2 1.9 %collective-permute-start.8 = (bf16[4,36,1152]{2,1,0:T(8,128)(2,1)S(1)}, bf16[4,36,1152]{2,1,0:T(8,128)(2,1)}, u32[]{:S(2)}, u32[]{:S(2)}) collective-permute-start(bf16[4,36,1152]{2,1,0:T(8,128)(2,1)S(1)} %pad_maximum_fusion.mine), channel_id=1, source_target_pairs={{0,64},{1,65},{2,66},{3,67},{4,68},{5,69},{6,70},{7,71},{8,72},{9,... | collective-permute-start | bytes 995336 | tf_op jit(solution)/shard_map/ppermute | solution.py:28
  50.1 4.7 %collective-permute-start.12 = (bf16[4,36,1152]{2,1,0:T(8,128)(2,1)S(1)}, bf16[4,36,1152]{2,1,0:T(8,128)(2,1)}, u32[]{:S(2)}, u32[]{:S(2)}) collective-permute-start(bf16[4,36,1152]{2,1,0:T(8,128)(2,1)S(1)} %pad_maximum_fusion.mine), channel_id=1, source_target_pairs={{0,32},{1,33},{2,34},{3,35},{4,36},{5,37},{6,38},{7,39},{8,40},{9,... | collective-permute-start | bytes 995336 | tf_op jit(solution)/shard_map/ppermute | solution.py:28
  54.8 0.0 collective-permute-done.3
  54.8 0.1 broadcast_select_fusion.im2
  54.9 0.0 collective-permute-done.8.other
  54.9 0.0 copy-done.4
  54.9 2.1 %shard_map.55.col = bf16[288,1152]{1,0:T(8,128)(2,1)} custom-call(bf16[4,36,1152]{2,1,0:T(8,128)(2,1)} %copy-done.4, bf16[4,36,1152]{2,1,0:T(8,128)(2,1)} %collective-permute-done.8.other), custom_call_target="tpu_custom_call" | custom-call | flops 331776 | bytes 1327104 | tf_op jit(solution)/shard_map/pallas_call | solution.py:57
  57.0 2.8 %collective-permute-start.11 = (bf16[288,1152]{1,0:T(8,128)(2,1)}, bf16[288,1152]{1,0:T(8,128)(2,1)}, u32[]{:S(2)}, u32[]{:S(2)}) collective-permute-start(bf16[288,1152]{1,0:T(8,128)(2,1)} %shard_map.55.col), channel_id=1, source_target_pairs={{0,16},{1,17},{2,18},{3,19},{4,20},{5,21},{6,22},{7,23},{8,24},{9,... | collective-permute-start | bytes 1990664 | tf_op jit(solution)/shard_map/ppermute | solution.py:28
  59.7 0.0 copy-done
  59.8 0.9 %broadcast_select_fusion.1 = bf16[256,1152]{1,0:T(8,128)(2,1)} fusion(bf16[256,1152]{1,0:T(8,128)(2,1)S(1)} %broadcast_select_fusion.im2, bf16[256,1152]{1,0:T(8,128)(2,1)S(1)} %copy-done, pred[]{:T(512)S(6)} %eq.7), kind=kLoop, calls=%fused_computation.1 | loop fusion | flops 294912 | bytes 1769473 | tf_op jit(solution)/shard_map/jit(_where)/select_n | solution.py:160
  60.6 2.4 %collective-permute-start.9 = (bf16[256,1152]{1,0:T(8,128)(2,1)}, bf16[256,1152]{1,0:T(8,128)(2,1)S(1)}, u32[]{:S(2)}, u32[]{:S(2)}) collective-permute-start(bf16[256,1152]{1,0:T(8,128)(2,1)} %broadcast_select_fusion.1), channel_id=1, source_target_pairs={{64,0},{65,1},{66,2},{67,3},{68,4},{69,5},{70,6},{71,7},{72,8},{73... | collective-permute-start | bytes 1769480 | tf_op jit(solution)/shard_map/ppermute | solution.py:28
  63.1 1.9 %collective-permute-start.10 = (bf16[256,1152]{1,0:T(8,128)(2,1)S(1)}, bf16[256,1152]{1,0:T(8,128)(2,1)S(1)}, u32[]{:S(2)}, u32[]{:S(2)}) collective-permute-start(bf16[256,1152]{1,0:T(8,128)(2,1)S(1)} %broadcast_select_fusion.im2), channel_id=1, source_target_pairs={{0,64},{1,65},{2,66},{3,67},{4,68},{5,69},{6,70},{7,71},{8,72},{9,... | collective-permute-start | bytes 1769480 | tf_op jit(solution)/shard_map/ppermute | solution.py:28
  65.0 0.0 collective-permute-done.12.mine
  65.0 2.4 %collective-permute-start.13 = (bf16[4,36,1152]{2,1,0:T(8,128)(2,1)}, bf16[4,36,1152]{2,1,0:T(8,128)(2,1)S(1)}, u32[]{:S(2)}, u32[]{:S(2)}) collective-permute-start(bf16[4,36,1152]{2,1,0:T(8,128)(2,1)} %collective-permute-done.12.mine), channel_id=1, source_target_pairs={{0,64},{1,65},{2,66},{3,67},{4,68},{5,69},{6,70},{7,71},{8,72},{9,... | collective-permute-start | bytes 995336 | tf_op jit(solution)/shard_map/ppermute | solution.py:28
  67.4 1.5 %collective-permute-done.13.other = bf16[4,36,1152]{2,1,0:T(8,128)(2,1)S(1)} collective-permute-done((bf16[4,36,1152]{2,1,0:T(8,128)(2,1)}, bf16[4,36,1152]{2,1,0:T(8,128)(2,1)S(1)}, u32[]{:S(2)}, u32[]{:S(2)}) %collective-permute-start.13) | collective-permute-done | bytes 331808 | tf_op jit(solution)/shard_map/ppermute | solution.py:28
  68.9 0.0 copy-start.5
  68.9 0.7 copy-done.5
  69.7 2.1 %shard_map.57.mcol = bf16[288,1152]{1,0:T(8,128)(2,1)} custom-call(bf16[4,36,1152]{2,1,0:T(8,128)(2,1)} %collective-permute-done.12.mine, bf16[4,36,1152]{2,1,0:T(8,128)(2,1)} %copy-done.5), custom_call_target="tpu_custom_call" | custom-call | flops 331776 | bytes 1327104 | tf_op jit(solution)/shard_map/pallas_call | solution.py:57
  71.7 3.9 %collective-permute-done.9.im1 = bf16[256,1152]{1,0:T(8,128)(2,1)S(1)} collective-permute-done((bf16[256,1152]{1,0:T(8,128)(2,1)}, bf16[256,1152]{1,0:T(8,128)(2,1)S(1)}, u32[]{:S(2)}, u32[]{:S(2)}) %collective-permute-start.9) | collective-permute-done | bytes 589856 | tf_op jit(solution)/shard_map/ppermute | solution.py:28
  75.6 0.0 collective-permute-done.10.im3
  75.6 0.0 collective-permute-done.11.xcol
  75.6 1.9 %collective-permute-start.14 = (bf16[288,1152]{1,0:T(8,128)(2,1)}, bf16[288,1152]{1,0:T(8,128)(2,1)}, u32[]{:S(2)}, u32[]{:S(2)}) collective-permute-start(bf16[288,1152]{1,0:T(8,128)(2,1)} %collective-permute-done.11.xcol), channel_id=1, source_target_pairs={{0,64},{1,65},{2,66},{3,67},{4,68},{5,69},{6,70},{7,71},{8,72},{9,... | collective-permute-start | bytes 1990664 | tf_op jit(solution)/shard_map/ppermute | solution.py:28
  78.9 0.1 pad_maximum_fusion.1.scal
  78.9 0.0 copy-start.1
  78.9 1.3 %shard_map.56.unit = bf16[1024,1152]{1,0:T(8,128)(2,1)S(1)} custom-call(bf16[256,1152]{1,0:T(8,128)(2,1)S(1)} %copy-done, bf16[256,1152]{1,0:T(8,128)(2,1)S(1)} %collective-permute-done.9.im1, bf16[256,1152]{1,0:T(8,128)(2,1)S(1)} %collective-permute-done.1.wrap, bf16[256,1152]{1,0:T(8,128)(2,1)S(1)} %broadcast_select_fusion.im2, ...), custom_call_target="tpu_custom_call" | custom-call | flops 3538944 | bytes 4718592 | tf_op jit(solution)/shard_map/pallas_call | solution.py:170
  80.3 0.0 collective-permute-done.14.ocol
  80.3 0.0 copy-done.1
  80.3 0.0 copy-done.2
  80.3 0.1 copy-done.3
  80.4 6.7 %shard_map.58 = bf16[256,1152]{1,0:T(8,128)(2,1)} custom-call(f32[2]{0:T(128)S(1)} %pad_maximum_fusion.1.scal, bf16[1024,1152]{1,0:T(8,128)(2,1)S(1)} %shard_map.56.unit, bf16[256,1152]{1,0:T(8,128)(2,1)S(1)} %copy-done.3, bf16[288,1152]{1,0:T(8,128)(2,1)S(1)} %copy-done.1, bf16[288,1152]{1,0:T(8,128)(2,1)} %collective-permute-done.11.xcol, ...), custom_call_target="tpu_custom_call" | custom-call | flops 2566914048 | bytes 8388608 | tf_op jit(solution)/shard_map/pallas_call | solution.py:185
  (5 shorter events, 0.1 us)
Async XLA Ops:
  0.0 59.7 %copy-start = (bf16[256,1152]{1,0:T(8,128)(2,1)S(1)}, bf16[256,1152]{1,0:T(8,128)(2,1)}, u32[]{:S(2)}) copy-start(bf16[256,1152]{1,0:T(8,128)(2,1)} %im0.1) | copy-start | bytes 1769476
  0.0 31.6 %collective-permute-start.2 = (bf16[18,1152]{1,0:T(8,128)(2,1)}, bf16[18,1152]{1,0:T(8,128)(2,1)S(1)}, u32[]{:S(2)}, u32[]{:S(2)}) collective-permute-start(bf16[18,1152]{1,0:T(8,128)(2,1)} %param.7), channel_id=1, source_target_pairs={{0,513},{1,512},{2,515},{3,514},{4,517},{5,516},{6,519},{7,518},{8... | collective-permute-start | bytes 124424 | tf_op jit(solution)/shard_map/ppermute | solution.py:28
  21.8 11.1 %collective-permute-start.4 = (bf16[18,1152]{1,0:T(8,128)(2,1)}, bf16[18,1152]{1,0:T(8,128)(2,1)S(1)}, u32[]{:S(2)}, u32[]{:S(2)}) collective-permute-start(bf16[18,1152]{1,0:T(8,128)(2,1)} %param.7), channel_id=1, source_target_pairs={{64,78},{65,79},{66,64},{67,65},{68,66},{69,67},{70,68},{71,69},{7... | collective-permute-start | bytes 124424 | tf_op jit(solution)/shard_map/ppermute | solution.py:28
  24.8 23.4 %collective-permute-start = (bf16[256,1152]{1,0:T(8,128)(2,1)}, bf16[256,1152]{1,0:T(8,128)(2,1)S(1)}, u32[]{:S(2)}, u32[]{:S(2)}) collective-permute-start(bf16[256,1152]{1,0:T(8,128)(2,1)} %im0.1), channel_id=1, source_target_pairs={{0,896},{1,897},{2,898},{3,899},{4,900},{5,901},{6,902},{7,903},{8... | collective-permute-start | bytes 1769480 | tf_op jit(solution)/shard_map/ppermute | solution.py:28
  30.9 17.3 %collective-permute-start.1 = (bf16[256,1152]{1,0:T(8,128)(2,1)}, bf16[256,1152]{1,0:T(8,128)(2,1)S(1)}, u32[]{:S(2)}, u32[]{:S(2)}) collective-permute-start(bf16[256,1152]{1,0:T(8,128)(2,1)} %im0.1), channel_id=1, source_target_pairs={{128,960},{129,961},{130,962},{131,963},{132,964},{133,965},{134,9... | collective-permute-start | bytes 1769480 | tf_op jit(solution)/shard_map/ppermute | solution.py:28
  31.6 23.2 %collective-permute-start.3 = (bf16[256,1152]{1,0:T(8,128)(2,1)}, bf16[256,1152]{1,0:T(8,128)(2,1)S(1)}, u32[]{:S(2)}, u32[]{:S(2)}) collective-permute-start(bf16[256,1152]{1,0:T(8,128)(2,1)} %im0.1), channel_id=1, source_target_pairs={{128,0},{129,1},{130,2},{131,3},{132,4},{133,5},{134,6},{135,7},{1... | collective-permute-start | bytes 1769480 | tf_op jit(solution)/shard_map/ppermute | solution.py:28
  33.0 7.7 %collective-permute-start.7 = (bf16[36,1152]{1,0:T(8,128)(2,1)S(1)}, bf16[36,1152]{1,0:T(8,128)(2,1)S(1)}, u32[]{:S(2)}, u32[]{:S(2)}) collective-permute-start(bf16[36,1152]{1,0:T(8,128)(2,1)S(1)} %maximum_select_fusion.1), channel_id=1, source_target_pairs={{0,6},{1,7},{2,8},{3,9},{4,10},{5,11},{6,12},{7,13},{8,14},{9,15},... | collective-permute-start | bytes 248840 | tf_op jit(solution)/shard_map/ppermute | solution.py:28
  36.7 9.9 %collective-permute-start.6 = (bf16[36,1152]{1,0:T(8,128)(2,1)S(1)}, bf16[36,1152]{1,0:T(8,128)(2,1)S(1)}, u32[]{:S(2)}, u32[]{:S(2)}) collective-permute-start(bf16[36,1152]{1,0:T(8,128)(2,1)S(1)} %maximum_select_fusion.1), channel_id=1, source_target_pairs={{0,4},{1,5},{2,6},{3,7},{4,8},{5,9},{6,10},{7,11},{8,12},{9,13},{1... | collective-permute-start | bytes 248840 | tf_op jit(solution)/shard_map/ppermute | solution.py:28
  40.7 7.4 %collective-permute-start.5 = (bf16[36,1152]{1,0:T(8,128)(2,1)S(1)}, bf16[36,1152]{1,0:T(8,128)(2,1)S(1)}, u32[]{:S(2)}, u32[]{:S(2)}) collective-permute-start(bf16[36,1152]{1,0:T(8,128)(2,1)S(1)} %maximum_select_fusion.1), channel_id=1, source_target_pairs={{0,2},{1,3},{2,4},{3,5},{4,6},{5,7},{6,8},{7,9},{8,10},{9,11},{10,... | collective-permute-start | bytes 248840 | tf_op jit(solution)/shard_map/ppermute | solution.py:28
  48.1 6.7 %copy-start.4 = (bf16[4,36,1152]{2,1,0:T(8,128)(2,1)}, bf16[4,36,1152]{2,1,0:T(8,128)(2,1)S(1)}, u32[]{:S(2)}) copy-start(bf16[4,36,1152]{2,1,0:T(8,128)(2,1)S(1)} %pad_maximum_fusion.mine) | copy-start | bytes 995332
  48.2 6.7 %collective-permute-start.8 = (bf16[4,36,1152]{2,1,0:T(8,128)(2,1)S(1)}, bf16[4,36,1152]{2,1,0:T(8,128)(2,1)}, u32[]{:S(2)}, u32[]{:S(2)}) collective-permute-start(bf16[4,36,1152]{2,1,0:T(8,128)(2,1)S(1)} %pad_maximum_fusion.mine), channel_id=1, source_target_pairs={{0,64},{1,65},{2,66},{3,67},{4,68},{5,69},{6,70},{7,71},{8,72},{9,... | collective-permute-start | bytes 995336 | tf_op jit(solution)/shard_map/ppermute | solution.py:28
  50.1 14.9 %collective-permute-start.12 = (bf16[4,36,1152]{2,1,0:T(8,128)(2,1)S(1)}, bf16[4,36,1152]{2,1,0:T(8,128)(2,1)}, u32[]{:S(2)}, u32[]{:S(2)}) collective-permute-start(bf16[4,36,1152]{2,1,0:T(8,128)(2,1)S(1)} %pad_maximum_fusion.mine), channel_id=1, source_target_pairs={{0,32},{1,33},{2,34},{3,35},{4,36},{5,37},{6,38},{7,39},{8,40},{9,... | collective-permute-start | bytes 995336 | tf_op jit(solution)/shard_map/ppermute | solution.py:28
  57.0 18.6 %collective-permute-start.11 = (bf16[288,1152]{1,0:T(8,128)(2,1)}, bf16[288,1152]{1,0:T(8,128)(2,1)}, u32[]{:S(2)}, u32[]{:S(2)}) collective-permute-start(bf16[288,1152]{1,0:T(8,128)(2,1)} %shard_map.55.col), channel_id=1, source_target_pairs={{0,16},{1,17},{2,18},{3,19},{4,20},{5,21},{6,22},{7,23},{8,24},{9,... | collective-permute-start | bytes 1990664 | tf_op jit(solution)/shard_map/ppermute | solution.py:28
  60.6 15.0 %collective-permute-start.9 = (bf16[256,1152]{1,0:T(8,128)(2,1)}, bf16[256,1152]{1,0:T(8,128)(2,1)S(1)}, u32[]{:S(2)}, u32[]{:S(2)}) collective-permute-start(bf16[256,1152]{1,0:T(8,128)(2,1)} %broadcast_select_fusion.1), channel_id=1, source_target_pairs={{64,0},{65,1},{66,2},{67,3},{68,4},{69,5},{70,6},{71,7},{72,8},{73... | collective-permute-start | bytes 1769480 | tf_op jit(solution)/shard_map/ppermute | solution.py:28
  63.1 12.6 %collective-permute-start.10 = (bf16[256,1152]{1,0:T(8,128)(2,1)S(1)}, bf16[256,1152]{1,0:T(8,128)(2,1)S(1)}, u32[]{:S(2)}, u32[]{:S(2)}) collective-permute-start(bf16[256,1152]{1,0:T(8,128)(2,1)S(1)} %broadcast_select_fusion.im2), channel_id=1, source_target_pairs={{0,64},{1,65},{2,66},{3,67},{4,68},{5,69},{6,70},{7,71},{8,72},{9,... | collective-permute-start | bytes 1769480 | tf_op jit(solution)/shard_map/ppermute | solution.py:28
  65.0 3.9 %collective-permute-start.13 = (bf16[4,36,1152]{2,1,0:T(8,128)(2,1)}, bf16[4,36,1152]{2,1,0:T(8,128)(2,1)S(1)}, u32[]{:S(2)}, u32[]{:S(2)}) collective-permute-start(bf16[4,36,1152]{2,1,0:T(8,128)(2,1)} %collective-permute-done.12.mine), channel_id=1, source_target_pairs={{0,64},{1,65},{2,66},{3,67},{4,68},{5,69},{6,70},{7,71},{8,72},{9,... | collective-permute-start | bytes 995336 | tf_op jit(solution)/shard_map/ppermute | solution.py:28
  68.9 0.7 copy-start.5
  75.6 4.7 %collective-permute-start.14 = (bf16[288,1152]{1,0:T(8,128)(2,1)}, bf16[288,1152]{1,0:T(8,128)(2,1)}, u32[]{:S(2)}, u32[]{:S(2)}) collective-permute-start(bf16[288,1152]{1,0:T(8,128)(2,1)} %collective-permute-done.11.xcol), channel_id=1, source_target_pairs={{0,64},{1,65},{2,66},{3,67},{4,68},{5,69},{6,70},{7,71},{8,72},{9,... | collective-permute-start | bytes 1990664 | tf_op jit(solution)/shard_map/ppermute | solution.py:28
  78.9 1.4 %copy-start.1 = (bf16[288,1152]{1,0:T(8,128)(2,1)S(1)}, bf16[288,1152]{1,0:T(8,128)(2,1)}, u32[]{:S(2)}) copy-start(bf16[288,1152]{1,0:T(8,128)(2,1)} %shard_map.55.col) | copy-start | bytes 1990660
  78.9 1.4 %copy-start.2 = (bf16[288,1152]{1,0:T(8,128)(2,1)S(1)}, bf16[288,1152]{1,0:T(8,128)(2,1)}, u32[]{:S(2)}) copy-start(bf16[288,1152]{1,0:T(8,128)(2,1)} %shard_map.57.mcol) | copy-start | bytes 1990660
  78.9 1.5 %copy-start.3 = (bf16[256,1152]{1,0:T(8,128)(2,1)S(1)}, bf16[256,1152]{1,0:T(8,128)(2,1)}, u32[]{:S(2)}) copy-start(bf16[256,1152]{1,0:T(8,128)(2,1)} %text.1) | copy-start | bytes 1769476

commit v4 on v3

--- a/solution.py
+++ b/solution.py
@@ -140,7 +140,6 @@
 
     wrap2 = moved(image_embed, lambda i, x, y, z: (i - 2, x, y, z) if i < 2 else None)
     wrap3 = moved(image_embed, lambda i, x, y, z: (i - 3, x, y, z) if i == 2 else None)
-    wrap2, wrap3 = lax.optimization_barrier((wrap2, wrap3))
     img = lax.optimization_barrier((image_embed, far))[0]
     near2 = moved(img, lambda i, x, y, z: (i - 2, x, y, z) if i >= 2 else None)
     two = jnp.where(isl >= n_isl - 2, wrap2, near2)
@@ -153,6 +152,7 @@
     mine = lax.optimization_barrier((mine, wrap2))[0]
     mid = moved(mine, lambda i, x, y, z: (i, x + 2, y, z))
     other = moved(mine, lambda i, x, y, z: (i ^ 1, x, y, z))
+    other = lax.optimization_barrier((other, wrap3))[0]
     col = column(mine, other)
     xcol = moved(col, lambda i, x, y, z: (i, x + (-1 if i % 2 else 1), y, z))
     two_ = lax.optimization_barrier((two, col))[0]

time: 87.7 us -> 83.8 us (0.956)
  waiting for transfers between devices: 8.86 us -> 6.15 us
  starting transfers between devices: 62.3 us -> 61.1 us
    ppermute x15, waiting for transfers between devices: 8.86 us -> 6.15 us  [moved(): return lax.ppermute(value, AXES, pairs)]
    ppermute x15, starting transfers between devices: 62.3 us -> 61.1 us  [moved(): return lax.ppermute(value, AXES, pairs)]
  transfers between devices with their start and end apart: 15 -> 15, of which waited for: 4 -> 4; matrix products, arithmetic and copies ran while one was open for 1% -> 1% of each run, Pallas kernels for 6% -> 7%
where the time goes in v4:
time: 83.8 us; the launch traced here: 83.2 us
  starting transfers between devices  61.1 us (73%)
  Pallas kernels  12.3 us (15%)
  waiting for transfers between devices  6.15 us (7%)
  between operations  1.62 us (2%)
  other arithmetic  1.22 us (1%)
  local copies, waits for them, and re-layouts  0.86 us (1%)
    ppermute x15, starting transfers between devices, moved(): return lax.ppermute(value, AXES, pairs)  61.1 us
    pallas_call x1, Pallas kernels, body(): pl.pallas_call(tail_kernel, out_shape=jax.ShapeDtypeStruct((rows, width),...  6.74 us
    ppermute x15, waiting for transfers between devices, moved(): return lax.ppermute(value, AXES, pairs)  6.15 us
    pallas_call x2, Pallas kernels, column(): pl.pallas_call(column_kernel, out_shape=jax.ShapeDtypeStruct((NY * 36, wi...  4.18 us
  transfers between devices with their start and end apart: 15, of which 4 were waited for; matrix products, arithmetic and copies ran while one was open for 1% of the time, Pallas kernels for 7%

profile of v4, /device:TPU:1, one launch (start us, length us, event | category | flops | bytes accessed | tf_op | source)
XLA Modules:
  0.0 83.2 jit_solution(10043856999475520428)
XLA Ops:
  0.0 0.0 copy-start
  0.0 21.8 %collective-permute-start.1 = (bf16[18,1152]{1,0:T(8,128)(2,1)}, bf16[18,1152]{1,0:T(8,128)(2,1)S(1)}, u32[]{:S(2)}, u32[]{:S(2)}) collective-permute-start(bf16[18,1152]{1,0:T(8,128)(2,1)} %param.7), channel_id=1, source_target_pairs={{0,513},{1,512},{2,515},{3,514},{4,517},{5,516},{6,519},{7,518},{8... | collective-permute-start | bytes 124424 | tf_op jit(solution)/shard_map/ppermute | solution.py:28
  21.8 3.0 %collective-permute-start.3 = (bf16[18,1152]{1,0:T(8,128)(2,1)}, bf16[18,1152]{1,0:T(8,128)(2,1)S(1)}, u32[]{:S(2)}, u32[]{:S(2)}) collective-permute-start(bf16[18,1152]{1,0:T(8,128)(2,1)} %param.7), channel_id=1, source_target_pairs={{64,78},{65,79},{66,64},{67,65},{68,66},{69,67},{70,68},{71,69},{7... | collective-permute-start | bytes 124424 | tf_op jit(solution)/shard_map/ppermute | solution.py:28
  24.8 6.1 %collective-permute-start = (bf16[256,1152]{1,0:T(8,128)(2,1)}, bf16[256,1152]{1,0:T(8,128)(2,1)S(1)}, u32[]{:S(2)}, u32[]{:S(2)}) collective-permute-start(bf16[256,1152]{1,0:T(8,128)(2,1)} %im0.1), channel_id=1, source_target_pairs={{0,896},{1,897},{2,898},{3,899},{4,900},{5,901},{6,902},{7,903},{8... | collective-permute-start | bytes 1769480 | tf_op jit(solution)/shard_map/ppermute | solution.py:28
  30.9 0.0 collective-permute-done.1
  30.9 1.3 %collective-permute-start.2 = (bf16[256,1152]{1,0:T(8,128)(2,1)}, bf16[256,1152]{1,0:T(8,128)(2,1)S(1)}, u32[]{:S(2)}, u32[]{:S(2)}) collective-permute-start(bf16[256,1152]{1,0:T(8,128)(2,1)} %im0.1), channel_id=1, source_target_pairs={{128,0},{129,1},{130,2},{131,3},{132,4},{133,5},{134,6},{135,7},{1... | collective-permute-start | bytes 1769480 | tf_op jit(solution)/shard_map/ppermute | solution.py:28
  32.2 0.0 collective-permute-done.3
  32.3 3.6 %collective-permute-start.6 = (bf16[36,1152]{1,0:T(8,128)(2,1)S(1)}, bf16[36,1152]{1,0:T(8,128)(2,1)S(1)}, u32[]{:S(2)}, u32[]{:S(2)}) collective-permute-start(bf16[36,1152]{1,0:T(8,128)(2,1)S(1)} %maximum_select_fusion.1), channel_id=1, source_target_pairs={{0,6},{1,7},{2,8},{3,9},{4,10},{5,11},{6,12},{7,13},{8,14},{9,15},... | collective-permute-start | bytes 248840 | tf_op jit(solution)/shard_map/ppermute | solution.py:28
  36.0 2.0 %collective-permute-start.5 = (bf16[36,1152]{1,0:T(8,128)(2,1)S(1)}, bf16[36,1152]{1,0:T(8,128)(2,1)S(1)}, u32[]{:S(2)}, u32[]{:S(2)}) collective-permute-start(bf16[36,1152]{1,0:T(8,128)(2,1)S(1)} %maximum_select_fusion.1), channel_id=1, source_target_pairs={{0,4},{1,5},{2,6},{3,7},{4,8},{5,9},{6,10},{7,11},{8,12},{9,13},{1... | collective-permute-start | bytes 248840 | tf_op jit(solution)/shard_map/ppermute | solution.py:28
  38.0 2.1 %collective-permute-start.4 = (bf16[36,1152]{1,0:T(8,128)(2,1)S(1)}, bf16[36,1152]{1,0:T(8,128)(2,1)S(1)}, u32[]{:S(2)}, u32[]{:S(2)}) collective-permute-start(bf16[36,1152]{1,0:T(8,128)(2,1)S(1)} %maximum_select_fusion.1), channel_id=1, source_target_pairs={{0,2},{1,3},{2,4},{3,5},{4,6},{5,7},{6,8},{7,9},{8,10},{9,11},{10,... | collective-permute-start | bytes 248840 | tf_op jit(solution)/shard_map/ppermute | solution.py:28
  40.1 0.0 collective-permute-done.6
  40.2 0.7 collective-permute-start.8
  40.9 2.6 %collective-permute-done.5 = bf16[36,1152]{1,0:T(8,128)(2,1)S(1)} collective-permute-done((bf16[36,1152]{1,0:T(8,128)(2,1)S(1)}, bf16[36,1152]{1,0:T(8,128)(2,1)S(1)}, u32[]{:S(2)}, u32[]{:S(2)}) %collective-permute-start.5) | collective-permute-done | bytes 82976 | tf_op jit(solution)/shard_map/ppermute | solution.py:28
  43.5 0.7 collective-permute-done.4
  44.2 0.1 pad_maximum_fusion.mine
  44.2 0.0 copy-start.4
  44.2 0.0 collective-permute-done
  44.3 4.9 %collective-permute-start.7 = (bf16[4,36,1152]{2,1,0:T(8,128)(2,1)S(1)}, bf16[4,36,1152]{2,1,0:T(8,128)(2,1)}, u32[]{:S(2)}, u32[]{:S(2)}) collective-permute-start(bf16[4,36,1152]{2,1,0:T(8,128)(2,1)S(1)} %pad_maximum_fusion.mine), channel_id=1, source_target_pairs={{0,64},{1,65},{2,66},{3,67},{4,68},{5,69},{6,70},{7,71},{8,72},{9,... | collective-permute-start | bytes 995336 | tf_op jit(solution)/shard_map/ppermute | solution.py:28
  49.1 4.7 %collective-permute-start.12 = (bf16[4,36,1152]{2,1,0:T(8,128)(2,1)S(1)}, bf16[4,36,1152]{2,1,0:T(8,128)(2,1)}, u32[]{:S(2)}, u32[]{:S(2)}) collective-permute-start(bf16[4,36,1152]{2,1,0:T(8,128)(2,1)S(1)} %pad_maximum_fusion.mine), channel_id=1, source_target_pairs={{0,32},{1,33},{2,34},{3,35},{4,36},{5,37},{6,38},{7,39},{8,40},{9,... | collective-permute-start | bytes 995336 | tf_op jit(solution)/shard_map/ppermute | solution.py:28
  53.8 0.0 collective-permute-done.2
  53.8 0.1 broadcast_select_fusion.im2
  53.9 0.0 collective-permute-done.8.wrap
  53.9 0.0 collective-permute-done.7.other
  53.9 0.0 copy-done.4
  53.9 2.1 %shard_map.55.col = bf16[288,1152]{1,0:T(8,128)(2,1)} custom-call(bf16[4,36,1152]{2,1,0:T(8,128)(2,1)} %copy-done.4, bf16[4,36,1152]{2,1,0:T(8,128)(2,1)} %collective-permute-done.7.other), custom_call_target="tpu_custom_call" | custom-call | flops 331776 | bytes 1327104 | tf_op jit(solution)/shard_map/pallas_call | solution.py:57
  56.0 2.8 %collective-permute-start.11 = (bf16[288,1152]{1,0:T(8,128)(2,1)}, bf16[288,1152]{1,0:T(8,128)(2,1)}, u32[]{:S(2)}, u32[]{:S(2)}) collective-permute-start(bf16[288,1152]{1,0:T(8,128)(2,1)} %shard_map.55.col), channel_id=1, source_target_pairs={{0,16},{1,17},{2,18},{3,19},{4,20},{5,21},{6,22},{7,23},{8,24},{9,... | collective-permute-start | bytes 1990664 | tf_op jit(solution)/shard_map/ppermute | solution.py:28
  58.8 0.0 copy-done
  58.8 0.9 %broadcast_select_fusion.1 = bf16[256,1152]{1,0:T(8,128)(2,1)} fusion(bf16[256,1152]{1,0:T(8,128)(2,1)S(1)} %broadcast_select_fusion.im2, bf16[256,1152]{1,0:T(8,128)(2,1)S(1)} %copy-done, pred[]{:T(512)S(6)} %eq.7), kind=kLoop, calls=%fused_computation.1 | loop fusion | flops 294912 | bytes 1769473 | tf_op jit(solution)/shard_map/jit(_where)/select_n | solution.py:160
  59.7 1.9 %collective-permute-start.9 = (bf16[256,1152]{1,0:T(8,128)(2,1)}, bf16[256,1152]{1,0:T(8,128)(2,1)S(1)}, u32[]{:S(2)}, u32[]{:S(2)}) collective-permute-start(bf16[256,1152]{1,0:T(8,128)(2,1)} %broadcast_select_fusion.1), channel_id=1, source_target_pairs={{64,0},{65,1},{66,2},{67,3},{68,4},{69,5},{70,6},{71,7},{72,8},{73... | collective-permute-start | bytes 1769480 | tf_op jit(solution)/shard_map/ppermute | solution.py:28
  61.6 1.9 %collective-permute-start.10 = (bf16[256,1152]{1,0:T(8,128)(2,1)S(1)}, bf16[256,1152]{1,0:T(8,128)(2,1)S(1)}, u32[]{:S(2)}, u32[]{:S(2)}) collective-permute-start(bf16[256,1152]{1,0:T(8,128)(2,1)S(1)} %broadcast_select_fusion.im2), channel_id=1, source_target_pairs={{0,64},{1,65},{2,66},{3,67},{4,68},{5,69},{6,70},{7,71},{8,72},{9,... | collective-permute-start | bytes 1769480 | tf_op jit(solution)/shard_map/ppermute | solution.py:28
  63.5 0.0 collective-permute-done.12.mine
  63.5 2.4 %collective-permute-start.13 = (bf16[4,36,1152]{2,1,0:T(8,128)(2,1)}, bf16[4,36,1152]{2,1,0:T(8,128)(2,1)S(1)}, u32[]{:S(2)}, u32[]{:S(2)}) collective-permute-start(bf16[4,36,1152]{2,1,0:T(8,128)(2,1)} %collective-permute-done.12.mine), channel_id=1, source_target_pairs={{0,64},{1,65},{2,66},{3,67},{4,68},{5,69},{6,70},{7,71},{8,72},{9,... | collective-permute-start | bytes 995336 | tf_op jit(solution)/shard_map/ppermute | solution.py:28
  66.0 1.5 %collective-permute-done.13.other = bf16[4,36,1152]{2,1,0:T(8,128)(2,1)S(1)} collective-permute-done((bf16[4,36,1152]{2,1,0:T(8,128)(2,1)}, bf16[4,36,1152]{2,1,0:T(8,128)(2,1)S(1)}, u32[]{:S(2)}, u32[]{:S(2)}) %collective-permute-start.13) | collective-permute-done | bytes 331808 | tf_op jit(solution)/shard_map/ppermute | solution.py:28
  67.5 0.0 copy-start.5
  67.5 0.7 copy-done.5
  68.2 2.1 %shard_map.57.mcol = bf16[288,1152]{1,0:T(8,128)(2,1)} custom-call(bf16[4,36,1152]{2,1,0:T(8,128)(2,1)} %collective-permute-done.12.mine, bf16[4,36,1152]{2,1,0:T(8,128)(2,1)} %copy-done.5), custom_call_target="tpu_custom_call" | custom-call | flops 331776 | bytes 1327104 | tf_op jit(solution)/shard_map/pallas_call | solution.py:57
  70.3 1.3 %collective-permute-done.9.im1 = bf16[256,1152]{1,0:T(8,128)(2,1)S(1)} collective-permute-done((bf16[256,1152]{1,0:T(8,128)(2,1)}, bf16[256,1152]{1,0:T(8,128)(2,1)S(1)}, u32[]{:S(2)}, u32[]{:S(2)}) %collective-permute-start.9) | collective-permute-done | bytes 589856 | tf_op jit(solution)/shard_map/ppermute | solution.py:28
  71.6 0.0 collective-permute-done.10.im3
  71.6 0.0 collective-permute-done.11.xcol
  71.6 1.9 %collective-permute-start.14 = (bf16[288,1152]{1,0:T(8,128)(2,1)}, bf16[288,1152]{1,0:T(8,128)(2,1)}, u32[]{:S(2)}, u32[]{:S(2)}) collective-permute-start(bf16[288,1152]{1,0:T(8,128)(2,1)} %collective-permute-done.11.xcol), channel_id=1, source_target_pairs={{0,64},{1,65},{2,66},{3,67},{4,68},{5,69},{6,70},{7,71},{8,72},{9,... | collective-permute-start | bytes 1990664 | tf_op jit(solution)/shard_map/ppermute | solution.py:28
  74.9 0.1 pad_maximum_fusion.1.scal
  75.0 0.0 copy-start.1
  75.0 1.3 %shard_map.56.unit = bf16[1024,1152]{1,0:T(8,128)(2,1)S(1)} custom-call(bf16[256,1152]{1,0:T(8,128)(2,1)S(1)} %copy-done, bf16[256,1152]{1,0:T(8,128)(2,1)S(1)} %collective-permute-done.9.im1, bf16[256,1152]{1,0:T(8,128)(2,1)S(1)} %collective-permute-done.8.wrap, bf16[256,1152]{1,0:T(8,128)(2,1)S(1)} %broadcast_select_fusion.im2, ...), custom_call_target="tpu_custom_call" | custom-call | flops 3538944 | bytes 4718592 | tf_op jit(solution)/shard_map/pallas_call | solution.py:170
  76.3 0.0 collective-permute-done.14.ocol
  76.3 0.0 copy-done.1
  76.3 0.0 copy-done.2
  76.3 0.1 copy-done.3
  76.4 6.7 %shard_map.58 = bf16[256,1152]{1,0:T(8,128)(2,1)} custom-call(f32[2]{0:T(128)S(1)} %pad_maximum_fusion.1.scal, bf16[1024,1152]{1,0:T(8,128)(2,1)S(1)} %shard_map.56.unit, bf16[256,1152]{1,0:T(8,128)(2,1)S(1)} %copy-done.3, bf16[288,1152]{1,0:T(8,128)(2,1)S(1)} %copy-done.1, bf16[288,1152]{1,0:T(8,128)(2,1)} %collective-permute-done.11.xcol, ...), custom_call_target="tpu_custom_call" | custom-call | flops 2566914048 | bytes 8388608 | tf_op jit(solution)/shard_map/pallas_call | solution.py:185
  (5 shorter events, 0.1 us)
Async XLA Ops:
  0.0 58.8 %copy-start = (bf16[256,1152]{1,0:T(8,128)(2,1)S(1)}, bf16[256,1152]{1,0:T(8,128)(2,1)}, u32[]{:S(2)}) copy-start(bf16[256,1152]{1,0:T(8,128)(2,1)} %im0.1) | copy-start | bytes 1769476
  0.0 30.9 %collective-permute-start.1 = (bf16[18,1152]{1,0:T(8,128)(2,1)}, bf16[18,1152]{1,0:T(8,128)(2,1)S(1)}, u32[]{:S(2)}, u32[]{:S(2)}) collective-permute-start(bf16[18,1152]{1,0:T(8,128)(2,1)} %param.7), channel_id=1, source_target_pairs={{0,513},{1,512},{2,515},{3,514},{4,517},{5,516},{6,519},{7,518},{8... | collective-permute-start | bytes 124424 | tf_op jit(solution)/shard_map/ppermute | solution.py:28
  21.8 10.4 %collective-permute-start.3 = (bf16[18,1152]{1,0:T(8,128)(2,1)}, bf16[18,1152]{1,0:T(8,128)(2,1)S(1)}, u32[]{:S(2)}, u32[]{:S(2)}) collective-permute-start(bf16[18,1152]{1,0:T(8,128)(2,1)} %param.7), channel_id=1, source_target_pairs={{64,78},{65,79},{66,64},{67,65},{68,66},{69,67},{70,68},{71,69},{7... | collective-permute-start | bytes 124424 | tf_op jit(solution)/shard_map/ppermute | solution.py:28
  24.8 19.5 %collective-permute-start = (bf16[256,1152]{1,0:T(8,128)(2,1)}, bf16[256,1152]{1,0:T(8,128)(2,1)S(1)}, u32[]{:S(2)}, u32[]{:S(2)}) collective-permute-start(bf16[256,1152]{1,0:T(8,128)(2,1)} %im0.1), channel_id=1, source_target_pairs={{0,896},{1,897},{2,898},{3,899},{4,900},{5,901},{6,902},{7,903},{8... | collective-permute-start | bytes 1769480 | tf_op jit(solution)/shard_map/ppermute | solution.py:28
  30.9 22.9 %collective-permute-start.2 = (bf16[256,1152]{1,0:T(8,128)(2,1)}, bf16[256,1152]{1,0:T(8,128)(2,1)S(1)}, u32[]{:S(2)}, u32[]{:S(2)}) collective-permute-start(bf16[256,1152]{1,0:T(8,128)(2,1)} %im0.1), channel_id=1, source_target_pairs={{128,0},{129,1},{130,2},{131,3},{132,4},{133,5},{134,6},{135,7},{1... | collective-permute-start | bytes 1769480 | tf_op jit(solution)/shard_map/ppermute | solution.py:28
  32.3 7.8 %collective-permute-start.6 = (bf16[36,1152]{1,0:T(8,128)(2,1)S(1)}, bf16[36,1152]{1,0:T(8,128)(2,1)S(1)}, u32[]{:S(2)}, u32[]{:S(2)}) collective-permute-start(bf16[36,1152]{1,0:T(8,128)(2,1)S(1)} %maximum_select_fusion.1), channel_id=1, source_target_pairs={{0,6},{1,7},{2,8},{3,9},{4,10},{5,11},{6,12},{7,13},{8,14},{9,15},... | collective-permute-start | bytes 248840 | tf_op jit(solution)/shard_map/ppermute | solution.py:28
  36.0 7.5 %collective-permute-start.5 = (bf16[36,1152]{1,0:T(8,128)(2,1)S(1)}, bf16[36,1152]{1,0:T(8,128)(2,1)S(1)}, u32[]{:S(2)}, u32[]{:S(2)}) collective-permute-start(bf16[36,1152]{1,0:T(8,128)(2,1)S(1)} %maximum_select_fusion.1), channel_id=1, source_target_pairs={{0,4},{1,5},{2,6},{3,7},{4,8},{5,9},{6,10},{7,11},{8,12},{9,13},{1... | collective-permute-start | bytes 248840 | tf_op jit(solution)/shard_map/ppermute | solution.py:28
  38.0 6.2 %collective-permute-start.4 = (bf16[36,1152]{1,0:T(8,128)(2,1)S(1)}, bf16[36,1152]{1,0:T(8,128)(2,1)S(1)}, u32[]{:S(2)}, u32[]{:S(2)}) collective-permute-start(bf16[36,1152]{1,0:T(8,128)(2,1)S(1)} %maximum_select_fusion.1), channel_id=1, source_target_pairs={{0,2},{1,3},{2,4},{3,5},{4,6},{5,7},{6,8},{7,9},{8,10},{9,11},{10,... | collective-permute-start | bytes 248840 | tf_op jit(solution)/shard_map/ppermute | solution.py:28
  40.2 13.7 %collective-permute-start.8 = (bf16[256,1152]{1,0:T(8,128)(2,1)}, bf16[256,1152]{1,0:T(8,128)(2,1)S(1)}, u32[]{:S(2)}, u32[]{:S(2)}) collective-permute-start(bf16[256,1152]{1,0:T(8,128)(2,1)} %im0.1), channel_id=1, source_target_pairs={{128,960},{129,961},{130,962},{131,963},{132,964},{133,965},{134,9... | collective-permute-start | bytes 1769480 | tf_op jit(solution)/shard_map/ppermute | solution.py:28
  44.2 9.7 %copy-start.4 = (bf16[4,36,1152]{2,1,0:T(8,128)(2,1)}, bf16[4,36,1152]{2,1,0:T(8,128)(2,1)S(1)}, u32[]{:S(2)}) copy-start(bf16[4,36,1152]{2,1,0:T(8,128)(2,1)S(1)} %pad_maximum_fusion.mine) | copy-start | bytes 995332
  44.3 9.6 %collective-permute-start.7 = (bf16[4,36,1152]{2,1,0:T(8,128)(2,1)S(1)}, bf16[4,36,1152]{2,1,0:T(8,128)(2,1)}, u32[]{:S(2)}, u32[]{:S(2)}) collective-permute-start(bf16[4,36,1152]{2,1,0:T(8,128)(2,1)S(1)} %pad_maximum_fusion.mine), channel_id=1, source_target_pairs={{0,64},{1,65},{2,66},{3,67},{4,68},{5,69},{6,70},{7,71},{8,72},{9,... | collective-permute-start | bytes 995336 | tf_op jit(solution)/shard_map/ppermute | solution.py:28
  49.1 14.4 %collective-permute-start.12 = (bf16[4,36,1152]{2,1,0:T(8,128)(2,1)S(1)}, bf16[4,36,1152]{2,1,0:T(8,128)(2,1)}, u32[]{:S(2)}, u32[]{:S(2)}) collective-permute-start(bf16[4,36,1152]{2,1,0:T(8,128)(2,1)S(1)} %pad_maximum_fusion.mine), channel_id=1, source_target_pairs={{0,32},{1,33},{2,34},{3,35},{4,36},{5,37},{6,38},{7,39},{8,40},{9,... | collective-permute-start | bytes 995336 | tf_op jit(solution)/shard_map/ppermute | solution.py:28
  56.0 15.6 %collective-permute-start.11 = (bf16[288,1152]{1,0:T(8,128)(2,1)}, bf16[288,1152]{1,0:T(8,128)(2,1)}, u32[]{:S(2)}, u32[]{:S(2)}) collective-permute-start(bf16[288,1152]{1,0:T(8,128)(2,1)} %shard_map.55.col), channel_id=1, source_target_pairs={{0,16},{1,17},{2,18},{3,19},{4,20},{5,21},{6,22},{7,23},{8,24},{9,... | collective-permute-start | bytes 1990664 | tf_op jit(solution)/shard_map/ppermute | solution.py:28
  59.7 11.9 %collective-permute-start.9 = (bf16[256,1152]{1,0:T(8,128)(2,1)}, bf16[256,1152]{1,0:T(8,128)(2,1)S(1)}, u32[]{:S(2)}, u32[]{:S(2)}) collective-permute-start(bf16[256,1152]{1,0:T(8,128)(2,1)} %broadcast_select_fusion.1), channel_id=1, source_target_pairs={{64,0},{65,1},{66,2},{67,3},{68,4},{69,5},{70,6},{71,7},{72,8},{73... | collective-permute-start | bytes 1769480 | tf_op jit(solution)/shard_map/ppermute | solution.py:28
  61.6 10.0 %collective-permute-start.10 = (bf16[256,1152]{1,0:T(8,128)(2,1)S(1)}, bf16[256,1152]{1,0:T(8,128)(2,1)S(1)}, u32[]{:S(2)}, u32[]{:S(2)}) collective-permute-start(bf16[256,1152]{1,0:T(8,128)(2,1)S(1)} %broadcast_select_fusion.im2), channel_id=1, source_target_pairs={{0,64},{1,65},{2,66},{3,67},{4,68},{5,69},{6,70},{7,71},{8,72},{9,... | collective-permute-start | bytes 1769480 | tf_op jit(solution)/shard_map/ppermute | solution.py:28
  63.5 3.9 %collective-permute-start.13 = (bf16[4,36,1152]{2,1,0:T(8,128)(2,1)}, bf16[4,36,1152]{2,1,0:T(8,128)(2,1)S(1)}, u32[]{:S(2)}, u32[]{:S(2)}) collective-permute-start(bf16[4,36,1152]{2,1,0:T(8,128)(2,1)} %collective-permute-done.12.mine), channel_id=1, source_target_pairs={{0,64},{1,65},{2,66},{3,67},{4,68},{5,69},{6,70},{7,71},{8,72},{9,... | collective-permute-start | bytes 995336 | tf_op jit(solution)/shard_map/ppermute | solution.py:28
  67.5 0.7 copy-start.5
  71.6 4.7 %collective-permute-start.14 = (bf16[288,1152]{1,0:T(8,128)(2,1)}, bf16[288,1152]{1,0:T(8,128)(2,1)}, u32[]{:S(2)}, u32[]{:S(2)}) collective-permute-start(bf16[288,1152]{1,0:T(8,128)(2,1)} %collective-permute-done.11.xcol), channel_id=1, source_target_pairs={{0,64},{1,65},{2,66},{3,67},{4,68},{5,69},{6,70},{7,71},{8,72},{9,... | collective-permute-start | bytes 1990664 | tf_op jit(solution)/shard_map/ppermute | solution.py:28
  75.0 1.4 %copy-start.1 = (bf16[288,1152]{1,0:T(8,128)(2,1)S(1)}, bf16[288,1152]{1,0:T(8,128)(2,1)}, u32[]{:S(2)}) copy-start(bf16[288,1152]{1,0:T(8,128)(2,1)} %shard_map.55.col) | copy-start | bytes 1990660
  75.0 1.4 %copy-start.2 = (bf16[288,1152]{1,0:T(8,128)(2,1)S(1)}, bf16[288,1152]{1,0:T(8,128)(2,1)}, u32[]{:S(2)}) copy-start(bf16[288,1152]{1,0:T(8,128)(2,1)} %shard_map.57.mcol) | copy-start | bytes 1990660
  75.0 1.5 %copy-start.3 = (bf16[256,1152]{1,0:T(8,128)(2,1)S(1)}, bf16[256,1152]{1,0:T(8,128)(2,1)}, u32[]{:S(2)}) copy-start(bf16[256,1152]{1,0:T(8,128)(2,1)} %text.1) | copy-start | bytes 1769476

commit v5 on v4

--- a/solution.py
+++ b/solution.py
@@ -152,7 +152,6 @@
     mine = lax.optimization_barrier((mine, wrap2))[0]
     mid = moved(mine, lambda i, x, y, z: (i, x + 2, y, z))
     other = moved(mine, lambda i, x, y, z: (i ^ 1, x, y, z))
-    other = lax.optimization_barrier((other, wrap3))[0]
     col = column(mine, other)
     xcol = moved(col, lambda i, x, y, z: (i, x + (-1 if i % 2 else 1), y, z))
     two_ = lax.optimization_barrier((two, col))[0]
@@ -164,7 +163,7 @@
     mid_ = mid
     omid = moved(mid_, lambda i, x, y, z: (i ^ 1, x, y, z))
     mcol = column(mid, omid)
-    xcol_ = lax.optimization_barrier((xcol, mcol, one, swapped))[0]
+    xcol_ = lax.optimization_barrier((xcol, mcol, one, swapped, wrap3))[0]
     ocol = moved(xcol_, lambda i, x, y, z: (i ^ 1, x, y, z))
 
     unit = pl.pallas_call(

time: 83.8 us -> 83.8 us (level)
  no operation moved by 1% of the time
where the time goes in v5:
time: 83.8 us; the launch traced here: 83.1 us
  starting transfers between devices  61.1 us (73%)
  Pallas kernels  12.2 us (15%)
  waiting for transfers between devices  6.15 us (7%)
  between operations  1.62 us (2%)
  other arithmetic  1.22 us (1%)
  local copies, waits for them, and re-layouts  0.86 us (1%)
    ppermute x15, starting transfers between devices, moved(): return lax.ppermute(value, AXES, pairs)  61.1 us
    pallas_call x1, Pallas kernels, body(): pl.pallas_call(tail_kernel, out_shape=jax.ShapeDtypeStruct((rows, width),...  6.72 us
    ppermute x15, waiting for transfers between devices, moved(): return lax.ppermute(value, AXES, pairs)  6.15 us
    pallas_call x2, Pallas kernels, column(): pl.pallas_call(column_kernel, out_shape=jax.ShapeDtypeStruct((NY * 36, wi...  4.18 us
  transfers between devices with their start and end apart: 15, of which 4 were waited for; matrix products, arithmetic and copies ran while one was open for 1% of the time, Pallas kernels for 7%

profile of v5, /device:TPU:1, one launch (start us, length us, event | category | flops | bytes accessed | tf_op | source)
XLA Modules:
  0.0 83.1 jit_solution(8150186529799090277)
XLA Ops:
  0.0 0.0 copy-start
  0.0 21.8 %collective-permute-start.1 = (bf16[18,1152]{1,0:T(8,128)(2,1)}, bf16[18,1152]{1,0:T(8,128)(2,1)S(1)}, u32[]{:S(2)}, u32[]{:S(2)}) collective-permute-start(bf16[18,1152]{1,0:T(8,128)(2,1)} %param.7), channel_id=1, source_target_pairs={{0,513},{1,512},{2,515},{3,514},{4,517},{5,516},{6,519},{7,518},{8... | collective-permute-start | bytes 124424 | tf_op jit(solution)/shard_map/ppermute | solution.py:28
  21.8 3.0 %collective-permute-start.3 = (bf16[18,1152]{1,0:T(8,128)(2,1)}, bf16[18,1152]{1,0:T(8,128)(2,1)S(1)}, u32[]{:S(2)}, u32[]{:S(2)}) collective-permute-start(bf16[18,1152]{1,0:T(8,128)(2,1)} %param.7), channel_id=1, source_target_pairs={{64,78},{65,79},{66,64},{67,65},{68,66},{69,67},{70,68},{71,69},{7... | collective-permute-start | bytes 124424 | tf_op jit(solution)/shard_map/ppermute | solution.py:28
  24.8 6.1 %collective-permute-start = (bf16[256,1152]{1,0:T(8,128)(2,1)}, bf16[256,1152]{1,0:T(8,128)(2,1)S(1)}, u32[]{:S(2)}, u32[]{:S(2)}) collective-permute-start(bf16[256,1152]{1,0:T(8,128)(2,1)} %im0.1), channel_id=1, source_target_pairs={{0,896},{1,897},{2,898},{3,899},{4,900},{5,901},{6,902},{7,903},{8... | collective-permute-start | bytes 1769480 | tf_op jit(solution)/shard_map/ppermute | solution.py:28
  30.9 0.0 collective-permute-done.1
  30.9 1.3 %collective-permute-start.2 = (bf16[256,1152]{1,0:T(8,128)(2,1)}, bf16[256,1152]{1,0:T(8,128)(2,1)S(1)}, u32[]{:S(2)}, u32[]{:S(2)}) collective-permute-start(bf16[256,1152]{1,0:T(8,128)(2,1)} %im0.1), channel_id=1, source_target_pairs={{128,0},{129,1},{130,2},{131,3},{132,4},{133,5},{134,6},{135,7},{1... | collective-permute-start | bytes 1769480 | tf_op jit(solution)/shard_map/ppermute | solution.py:28
  32.2 0.0 collective-permute-done.3
  32.3 3.6 %collective-permute-start.6 = (bf16[36,1152]{1,0:T(8,128)(2,1)S(1)}, bf16[36,1152]{1,0:T(8,128)(2,1)S(1)}, u32[]{:S(2)}, u32[]{:S(2)}) collective-permute-start(bf16[36,1152]{1,0:T(8,128)(2,1)S(1)} %maximum_select_fusion.1), channel_id=1, source_target_pairs={{0,6},{1,7},{2,8},{3,9},{4,10},{5,11},{6,12},{7,13},{8,14},{9,15},... | collective-permute-start | bytes 248840 | tf_op jit(solution)/shard_map/ppermute | solution.py:28
  36.0 2.0 %collective-permute-start.5 = (bf16[36,1152]{1,0:T(8,128)(2,1)S(1)}, bf16[36,1152]{1,0:T(8,128)(2,1)S(1)}, u32[]{:S(2)}, u32[]{:S(2)}) collective-permute-start(bf16[36,1152]{1,0:T(8,128)(2,1)S(1)} %maximum_select_fusion.1), channel_id=1, source_target_pairs={{0,4},{1,5},{2,6},{3,7},{4,8},{5,9},{6,10},{7,11},{8,12},{9,13},{1... | collective-permute-start | bytes 248840 | tf_op jit(solution)/shard_map/ppermute | solution.py:28
  38.0 2.1 %collective-permute-start.4 = (bf16[36,1152]{1,0:T(8,128)(2,1)S(1)}, bf16[36,1152]{1,0:T(8,128)(2,1)S(1)}, u32[]{:S(2)}, u32[]{:S(2)}) collective-permute-start(bf16[36,1152]{1,0:T(8,128)(2,1)S(1)} %maximum_select_fusion.1), channel_id=1, source_target_pairs={{0,2},{1,3},{2,4},{3,5},{4,6},{5,7},{6,8},{7,9},{8,10},{9,11},{10,... | collective-permute-start | bytes 248840 | tf_op jit(solution)/shard_map/ppermute | solution.py:28
  40.1 0.0 collective-permute-done.6
  40.2 0.7 collective-permute-start.9
  40.9 2.6 %collective-permute-done.5 = bf16[36,1152]{1,0:T(8,128)(2,1)S(1)} collective-permute-done((bf16[36,1152]{1,0:T(8,128)(2,1)S(1)}, bf16[36,1152]{1,0:T(8,128)(2,1)S(1)}, u32[]{:S(2)}, u32[]{:S(2)}) %collective-permute-start.5) | collective-permute-done | bytes 82976 | tf_op jit(solution)/shard_map/ppermute | solution.py:28
  43.5 0.7 collective-permute-done.4
  44.2 0.1 pad_maximum_fusion.mine
  44.2 0.0 copy-start.4
  44.2 0.0 collective-permute-done
  44.3 4.9 %collective-permute-start.7 = (bf16[4,36,1152]{2,1,0:T(8,128)(2,1)S(1)}, bf16[4,36,1152]{2,1,0:T(8,128)(2,1)}, u32[]{:S(2)}, u32[]{:S(2)}) collective-permute-start(bf16[4,36,1152]{2,1,0:T(8,128)(2,1)S(1)} %pad_maximum_fusion.mine), channel_id=1, source_target_pairs={{0,64},{1,65},{2,66},{3,67},{4,68},{5,69},{6,70},{7,71},{8,72},{9,... | collective-permute-start | bytes 995336 | tf_op jit(solution)/shard_map/ppermute | solution.py:28
  49.1 4.7 %collective-permute-start.12 = (bf16[4,36,1152]{2,1,0:T(8,128)(2,1)S(1)}, bf16[4,36,1152]{2,1,0:T(8,128)(2,1)}, u32[]{:S(2)}, u32[]{:S(2)}) collective-permute-start(bf16[4,36,1152]{2,1,0:T(8,128)(2,1)S(1)} %pad_maximum_fusion.mine), channel_id=1, source_target_pairs={{0,32},{1,33},{2,34},{3,35},{4,36},{5,37},{6,38},{7,39},{8,40},{9,... | collective-permute-start | bytes 995336 | tf_op jit(solution)/shard_map/ppermute | solution.py:28
  53.8 0.0 collective-permute-done.2
  53.8 0.1 broadcast_select_fusion.im2
  53.9 0.0 collective-permute-done.7.other
  53.9 0.0 copy-done.4
  53.9 2.1 %shard_map.55.col = bf16[288,1152]{1,0:T(8,128)(2,1)} custom-call(bf16[4,36,1152]{2,1,0:T(8,128)(2,1)} %copy-done.4, bf16[4,36,1152]{2,1,0:T(8,128)(2,1)} %collective-permute-done.7.other), custom_call_target="tpu_custom_call" | custom-call | flops 331776 | bytes 1327104 | tf_op jit(solution)/shard_map/pallas_call | solution.py:57
  56.0 2.8 %collective-permute-start.11 = (bf16[288,1152]{1,0:T(8,128)(2,1)}, bf16[288,1152]{1,0:T(8,128)(2,1)}, u32[]{:S(2)}, u32[]{:S(2)}) collective-permute-start(bf16[288,1152]{1,0:T(8,128)(2,1)} %shard_map.55.col), channel_id=1, source_target_pairs={{0,16},{1,17},{2,18},{3,19},{4,20},{5,21},{6,22},{7,23},{8,24},{9,... | collective-permute-start | bytes 1990664 | tf_op jit(solution)/shard_map/ppermute | solution.py:28
  58.8 0.0 copy-done
  58.8 0.9 %broadcast_select_fusion.1 = bf16[256,1152]{1,0:T(8,128)(2,1)} fusion(bf16[256,1152]{1,0:T(8,128)(2,1)S(1)} %broadcast_select_fusion.im2, bf16[256,1152]{1,0:T(8,128)(2,1)S(1)} %copy-done, pred[]{:T(512)S(6)} %eq.7), kind=kLoop, calls=%fused_computation.1 | loop fusion | flops 294912 | bytes 1769473 | tf_op jit(solution)/shard_map/jit(_where)/select_n | solution.py:159
  59.7 1.9 %collective-permute-start.8 = (bf16[256,1152]{1,0:T(8,128)(2,1)}, bf16[256,1152]{1,0:T(8,128)(2,1)S(1)}, u32[]{:S(2)}, u32[]{:S(2)}) collective-permute-start(bf16[256,1152]{1,0:T(8,128)(2,1)} %broadcast_select_fusion.1), channel_id=1, source_target_pairs={{64,0},{65,1},{66,2},{67,3},{68,4},{69,5},{70,6},{71,7},{72,8},{73... | collective-permute-start | bytes 1769480 | tf_op jit(solution)/shard_map/ppermute | solution.py:28
  61.6 1.9 %collective-permute-start.10 = (bf16[256,1152]{1,0:T(8,128)(2,1)S(1)}, bf16[256,1152]{1,0:T(8,128)(2,1)S(1)}, u32[]{:S(2)}, u32[]{:S(2)}) collective-permute-start(bf16[256,1152]{1,0:T(8,128)(2,1)S(1)} %broadcast_select_fusion.im2), channel_id=1, source_target_pairs={{0,64},{1,65},{2,66},{3,67},{4,68},{5,69},{6,70},{7,71},{8,72},{9,... | collective-permute-start | bytes 1769480 | tf_op jit(solution)/shard_map/ppermute | solution.py:28
  63.5 0.0 collective-permute-done.12.mine
  63.5 2.4 %collective-permute-start.13 = (bf16[4,36,1152]{2,1,0:T(8,128)(2,1)}, bf16[4,36,1152]{2,1,0:T(8,128)(2,1)S(1)}, u32[]{:S(2)}, u32[]{:S(2)}) collective-permute-start(bf16[4,36,1152]{2,1,0:T(8,128)(2,1)} %collective-permute-done.12.mine), channel_id=1, source_target_pairs={{0,64},{1,65},{2,66},{3,67},{4,68},{5,69},{6,70},{7,71},{8,72},{9,... | collective-permute-start | bytes 995336 | tf_op jit(solution)/shard_map/ppermute | solution.py:28
  65.9 1.5 %collective-permute-done.13.other = bf16[4,36,1152]{2,1,0:T(8,128)(2,1)S(1)} collective-permute-done((bf16[4,36,1152]{2,1,0:T(8,128)(2,1)}, bf16[4,36,1152]{2,1,0:T(8,128)(2,1)S(1)}, u32[]{:S(2)}, u32[]{:S(2)}) %collective-permute-start.13) | collective-permute-done | bytes 331808 | tf_op jit(solution)/shard_map/ppermute | solution.py:28
  67.4 0.0 copy-start.5
  67.4 0.7 copy-done.5
  68.2 2.1 %shard_map.57.mcol = bf16[288,1152]{1,0:T(8,128)(2,1)} custom-call(bf16[4,36,1152]{2,1,0:T(8,128)(2,1)} %collective-permute-done.12.mine, bf16[4,36,1152]{2,1,0:T(8,128)(2,1)} %copy-done.5), custom_call_target="tpu_custom_call" | custom-call | flops 331776 | bytes 1327104 | tf_op jit(solution)/shard_map/pallas_call | solution.py:57
  70.3 0.0 collective-permute-done.9.wrap
  70.3 1.3 %collective-permute-done.8.im1 = bf16[256,1152]{1,0:T(8,128)(2,1)S(1)} collective-permute-done((bf16[256,1152]{1,0:T(8,128)(2,1)}, bf16[256,1152]{1,0:T(8,128)(2,1)S(1)}, u32[]{:S(2)}, u32[]{:S(2)}) %collective-permute-start.8) | collective-permute-done | bytes 589856 | tf_op jit(solution)/shard_map/ppermute | solution.py:28
  71.6 0.0 collective-permute-done.10.im3
  71.6 0.0 collective-permute-done.11.xcol
  71.6 1.9 %collective-permute-start.14 = (bf16[288,1152]{1,0:T(8,128)(2,1)}, bf16[288,1152]{1,0:T(8,128)(2,1)}, u32[]{:S(2)}, u32[]{:S(2)}) collective-permute-start(bf16[288,1152]{1,0:T(8,128)(2,1)} %collective-permute-done.11.xcol), channel_id=1, source_target_pairs={{0,64},{1,65},{2,66},{3,67},{4,68},{5,69},{6,70},{7,71},{8,72},{9,... | collective-permute-start | bytes 1990664 | tf_op jit(solution)/shard_map/ppermute | solution.py:28
  74.9 0.1 pad_maximum_fusion.1.scal
  74.9 0.0 copy-start.1
  74.9 1.3 %shard_map.56.unit = bf16[1024,1152]{1,0:T(8,128)(2,1)S(1)} custom-call(bf16[256,1152]{1,0:T(8,128)(2,1)S(1)} %copy-done, bf16[256,1152]{1,0:T(8,128)(2,1)S(1)} %collective-permute-done.8.im1, bf16[256,1152]{1,0:T(8,128)(2,1)S(1)} %collective-permute-done.9.wrap, bf16[256,1152]{1,0:T(8,128)(2,1)S(1)} %broadcast_select_fusion.im2, ...), custom_call_target="tpu_custom_call" | custom-call | flops 3538944 | bytes 4718592 | tf_op jit(solution)/shard_map/pallas_call | solution.py:169
  76.3 0.0 collective-permute-done.14.ocol
  76.3 0.0 copy-done.1
  76.3 0.0 copy-done.2
  76.3 0.1 copy-done.3
  76.4 6.7 %shard_map.58 = bf16[256,1152]{1,0:T(8,128)(2,1)} custom-call(f32[2]{0:T(128)S(1)} %pad_maximum_fusion.1.scal, bf16[1024,1152]{1,0:T(8,128)(2,1)S(1)} %shard_map.56.unit, bf16[256,1152]{1,0:T(8,128)(2,1)S(1)} %copy-done.3, bf16[288,1152]{1,0:T(8,128)(2,1)S(1)} %copy-done.1, bf16[288,1152]{1,0:T(8,128)(2,1)} %collective-permute-done.11.xcol, ...), custom_call_target="tpu_custom_call" | custom-call | flops 2566914048 | bytes 8388608 | tf_op jit(solution)/shard_map/pallas_call | solution.py:184
  (5 shorter events, 0.1 us)
Async XLA Ops:
  0.0 58.8 %copy-start = (bf16[256,1152]{1,0:T(8,128)(2,1)S(1)}, bf16[256,1152]{1,0:T(8,128)(2,1)}, u32[]{:S(2)}) copy-start(bf16[256,1152]{1,0:T(8,128)(2,1)} %im0.1) | copy-start | bytes 1769476
  0.0 30.9 %collective-permute-start.1 = (bf16[18,1152]{1,0:T(8,128)(2,1)}, bf16[18,1152]{1,0:T(8,128)(2,1)S(1)}, u32[]{:S(2)}, u32[]{:S(2)}) collective-permute-start(bf16[18,1152]{1,0:T(8,128)(2,1)} %param.7), channel_id=1, source_target_pairs={{0,513},{1,512},{2,515},{3,514},{4,517},{5,516},{6,519},{7,518},{8... | collective-permute-start | bytes 124424 | tf_op jit(solution)/shard_map/ppermute | solution.py:28
  21.8 10.4 %collective-permute-start.3 = (bf16[18,1152]{1,0:T(8,128)(2,1)}, bf16[18,1152]{1,0:T(8,128)(2,1)S(1)}, u32[]{:S(2)}, u32[]{:S(2)}) collective-permute-start(bf16[18,1152]{1,0:T(8,128)(2,1)} %param.7), channel_id=1, source_target_pairs={{64,78},{65,79},{66,64},{67,65},{68,66},{69,67},{70,68},{71,69},{7... | collective-permute-start | bytes 124424 | tf_op jit(solution)/shard_map/ppermute | solution.py:28
  24.8 19.5 %collective-permute-start = (bf16[256,1152]{1,0:T(8,128)(2,1)}, bf16[256,1152]{1,0:T(8,128)(2,1)S(1)}, u32[]{:S(2)}, u32[]{:S(2)}) collective-permute-start(bf16[256,1152]{1,0:T(8,128)(2,1)} %im0.1), channel_id=1, source_target_pairs={{0,896},{1,897},{2,898},{3,899},{4,900},{5,901},{6,902},{7,903},{8... | collective-permute-start | bytes 1769480 | tf_op jit(solution)/shard_map/ppermute | solution.py:28
  30.9 22.9 %collective-permute-start.2 = (bf16[256,1152]{1,0:T(8,128)(2,1)}, bf16[256,1152]{1,0:T(8,128)(2,1)S(1)}, u32[]{:S(2)}, u32[]{:S(2)}) collective-permute-start(bf16[256,1152]{1,0:T(8,128)(2,1)} %im0.1), channel_id=1, source_target_pairs={{128,0},{129,1},{130,2},{131,3},{132,4},{133,5},{134,6},{135,7},{1... | collective-permute-start | bytes 1769480 | tf_op jit(solution)/shard_map/ppermute | solution.py:28
  32.3 7.8 %collective-permute-start.6 = (bf16[36,1152]{1,0:T(8,128)(2,1)S(1)}, bf16[36,1152]{1,0:T(8,128)(2,1)S(1)}, u32[]{:S(2)}, u32[]{:S(2)}) collective-permute-start(bf16[36,1152]{1,0:T(8,128)(2,1)S(1)} %maximum_select_fusion.1), channel_id=1, source_target_pairs={{0,6},{1,7},{2,8},{3,9},{4,10},{5,11},{6,12},{7,13},{8,14},{9,15},... | collective-permute-start | bytes 248840 | tf_op jit(solution)/shard_map/ppermute | solution.py:28
  36.0 7.5 %collective-permute-start.5 = (bf16[36,1152]{1,0:T(8,128)(2,1)S(1)}, bf16[36,1152]{1,0:T(8,128)(2,1)S(1)}, u32[]{:S(2)}, u32[]{:S(2)}) collective-permute-start(bf16[36,1152]{1,0:T(8,128)(2,1)S(1)} %maximum_select_fusion.1), channel_id=1, source_target_pairs={{0,4},{1,5},{2,6},{3,7},{4,8},{5,9},{6,10},{7,11},{8,12},{9,13},{1... | collective-permute-start | bytes 248840 | tf_op jit(solution)/shard_map/ppermute | solution.py:28
  38.0 6.2 %collective-permute-start.4 = (bf16[36,1152]{1,0:T(8,128)(2,1)S(1)}, bf16[36,1152]{1,0:T(8,128)(2,1)S(1)}, u32[]{:S(2)}, u32[]{:S(2)}) collective-permute-start(bf16[36,1152]{1,0:T(8,128)(2,1)S(1)} %maximum_select_fusion.1), channel_id=1, source_target_pairs={{0,2},{1,3},{2,4},{3,5},{4,6},{5,7},{6,8},{7,9},{8,10},{9,11},{10,... | collective-permute-start | bytes 248840 | tf_op jit(solution)/shard_map/ppermute | solution.py:28
  40.2 30.1 %collective-permute-start.9 = (bf16[256,1152]{1,0:T(8,128)(2,1)}, bf16[256,1152]{1,0:T(8,128)(2,1)S(1)}, u32[]{:S(2)}, u32[]{:S(2)}) collective-permute-start(bf16[256,1152]{1,0:T(8,128)(2,1)} %im0.1), channel_id=1, source_target_pairs={{128,960},{129,961},{130,962},{131,963},{132,964},{133,965},{134,9... | collective-permute-start | bytes 1769480 | tf_op jit(solution)/shard_map/ppermute | solution.py:28
  44.2 9.7 %copy-start.4 = (bf16[4,36,1152]{2,1,0:T(8,128)(2,1)}, bf16[4,36,1152]{2,1,0:T(8,128)(2,1)S(1)}, u32[]{:S(2)}) copy-start(bf16[4,36,1152]{2,1,0:T(8,128)(2,1)S(1)} %pad_maximum_fusion.mine) | copy-start | bytes 995332
  44.3 9.6 %collective-permute-start.7 = (bf16[4,36,1152]{2,1,0:T(8,128)(2,1)S(1)}, bf16[4,36,1152]{2,1,0:T(8,128)(2,1)}, u32[]{:S(2)}, u32[]{:S(2)}) collective-permute-start(bf16[4,36,1152]{2,1,0:T(8,128)(2,1)S(1)} %pad_maximum_fusion.mine), channel_id=1, source_target_pairs={{0,64},{1,65},{2,66},{3,67},{4,68},{5,69},{6,70},{7,71},{8,72},{9,... | collective-permute-start | bytes 995336 | tf_op jit(solution)/shard_map/ppermute | solution.py:28
  49.1 14.4 %collective-permute-start.12 = (bf16[4,36,1152]{2,1,0:T(8,128)(2,1)S(1)}, bf16[4,36,1152]{2,1,0:T(8,128)(2,1)}, u32[]{:S(2)}, u32[]{:S(2)}) collective-permute-start(bf16[4,36,1152]{2,1,0:T(8,128)(2,1)S(1)} %pad_maximum_fusion.mine), channel_id=1, source_target_pairs={{0,32},{1,33},{2,34},{3,35},{4,36},{5,37},{6,38},{7,39},{8,40},{9,... | collective-permute-start | bytes 995336 | tf_op jit(solution)/shard_map/ppermute | solution.py:28
  56.0 15.6 %collective-permute-start.11 = (bf16[288,1152]{1,0:T(8,128)(2,1)}, bf16[288,1152]{1,0:T(8,128)(2,1)}, u32[]{:S(2)}, u32[]{:S(2)}) collective-permute-start(bf16[288,1152]{1,0:T(8,128)(2,1)} %shard_map.55.col), channel_id=1, source_target_pairs={{0,16},{1,17},{2,18},{3,19},{4,20},{5,21},{6,22},{7,23},{8,24},{9,... | collective-permute-start | bytes 1990664 | tf_op jit(solution)/shard_map/ppermute | solution.py:28
  59.7 11.9 %collective-permute-start.8 = (bf16[256,1152]{1,0:T(8,128)(2,1)}, bf16[256,1152]{1,0:T(8,128)(2,1)S(1)}, u32[]{:S(2)}, u32[]{:S(2)}) collective-permute-start(bf16[256,1152]{1,0:T(8,128)(2,1)} %broadcast_select_fusion.1), channel_id=1, source_target_pairs={{64,0},{65,1},{66,2},{67,3},{68,4},{69,5},{70,6},{71,7},{72,8},{73... | collective-permute-start | bytes 1769480 | tf_op jit(solution)/shard_map/ppermute | solution.py:28
  61.6 10.0 %collective-permute-start.10 = (bf16[256,1152]{1,0:T(8,128)(2,1)S(1)}, bf16[256,1152]{1,0:T(8,128)(2,1)S(1)}, u32[]{:S(2)}, u32[]{:S(2)}) collective-permute-start(bf16[256,1152]{1,0:T(8,128)(2,1)S(1)} %broadcast_select_fusion.im2), channel_id=1, source_target_pairs={{0,64},{1,65},{2,66},{3,67},{4,68},{5,69},{6,70},{7,71},{8,72},{9,... | collective-permute-start | bytes 1769480 | tf_op jit(solution)/shard_map/ppermute | solution.py:28
  63.5 3.9 %collective-permute-start.13 = (bf16[4,36,1152]{2,1,0:T(8,128)(2,1)}, bf16[4,36,1152]{2,1,0:T(8,128)(2,1)S(1)}, u32[]{:S(2)}, u32[]{:S(2)}) collective-permute-start(bf16[4,36,1152]{2,1,0:T(8,128)(2,1)} %collective-permute-done.12.mine), channel_id=1, source_target_pairs={{0,64},{1,65},{2,66},{3,67},{4,68},{5,69},{6,70},{7,71},{8,72},{9,... | collective-permute-start | bytes 995336 | tf_op jit(solution)/shard_map/ppermute | solution.py:28
  67.4 0.7 copy-start.5
  71.6 4.7 %collective-permute-start.14 = (bf16[288,1152]{1,0:T(8,128)(2,1)}, bf16[288,1152]{1,0:T(8,128)(2,1)}, u32[]{:S(2)}, u32[]{:S(2)}) collective-permute-start(bf16[288,1152]{1,0:T(8,128)(2,1)} %collective-permute-done.11.xcol), channel_id=1, source_target_pairs={{0,64},{1,65},{2,66},{3,67},{4,68},{5,69},{6,70},{7,71},{8,72},{9,... | collective-permute-start | bytes 1990664 | tf_op jit(solution)/shard_map/ppermute | solution.py:28
  74.9 1.4 %copy-start.1 = (bf16[288,1152]{1,0:T(8,128)(2,1)S(1)}, bf16[288,1152]{1,0:T(8,128)(2,1)}, u32[]{:S(2)}) copy-start(bf16[288,1152]{1,0:T(8,128)(2,1)} %shard_map.55.col) | copy-start | bytes 1990660
  74.9 1.4 %copy-start.2 = (bf16[288,1152]{1,0:T(8,128)(2,1)S(1)}, bf16[288,1152]{1,0:T(8,128)(2,1)}, u32[]{:S(2)}) copy-start(bf16[288,1152]{1,0:T(8,128)(2,1)} %shard_map.57.mcol) | copy-start | bytes 1990660
  74.9 1.5 %copy-start.3 = (bf16[256,1152]{1,0:T(8,128)(2,1)S(1)}, bf16[256,1152]{1,0:T(8,128)(2,1)}, u32[]{:S(2)}) copy-start(bf16[256,1152]{1,0:T(8,128)(2,1)} %text.1) | copy-start | bytes 1769476
